TPU v7x, 256 devices: a whole 4x4x8 slice. The times are simulated.
256 devices in a mesh: row: 32 (over y_lo, z, core), col: 8 (over y_hi, x).
Axes of the slice: x: 4, y: 4 (y_hi: 2, y_lo: 2; y = y_hi * 2 + y_lo), z: 8, core: 2. Of those that a mesh axis runs over, the one named last changes fastest.
Arguments:
- features: bfloat16 [768, 256, 256], P('row', 'col'), may hold values from -6 to 6
- grad_out: bfloat16 [768, 256, 256], P('row', 'col'), may hold values from -6 to 6
- weight: bfloat16 [9, 256, 256], replicated, may hold values from -0.125 to 0.125
- sample_taps: int32 [2, 9, 768, 256], P(None, None, 'row', 'col'), may hold values from 0 to 766, as said below
- fraction: float32 [2, 9, 768, 256], P(None, None, 'row', 'col'), may hold values from 0 to 1
- modulation: float32 [9, 768, 256], P(None, 'row', 'col'), may hold values from 0.2 to 1
Outputs:
- grad_x: bfloat16 [768, 256, 256], P('row', 'col')
- grad_w: float32 [256, 2304], P('col', 'row')
Inputs may be any that keep to these rules, and one draw needn't show every extreme that they name: `sample_taps`: the 2 x 2 cell lies inside the map, and both its rows lie within 17 rows, both its columns within 17 columns, of its pixel.
All inputs are finite; a program needn't handle non-finite values.
Results may differ from a plain program's by a relative error of at most 0.009.
Values may be sent and summed in bfloat16 or wider, within the bound.
A program may use at most 128 MiB of HBM per device.

v0:
```python
import math

import jax
import jax.numpy as jnp
from jax import lax
from jax.sharding import PartitionSpec as P

BOUND = 16


def from_behind(shard, axis, by):
    devices = lax.axis_size(axis)
    pairs = [(i, i + by) for i in range(devices) if 0 <= i + by < devices]
    return lax.ppermute(shard, axis, pairs)


def with_halo(shard, sides, width):
    for axis, dim in sides:
        devices, length = (lax.axis_size(axis), shard.shape[dim])
        up = [(i, (i + 1) % devices) for i in range(devices - 1)]
        down = [(j, i) for i, j in up]
        last = lax.slice_in_dim(shard, length - width, length, axis=dim)
        leading = lax.slice_in_dim(shard, 0, width, axis=dim)
        before = lax.ppermute(last, axis, up)
        after = lax.ppermute(leading, axis, down)
        shard = jnp.concatenate([before, shard, after], axis=dim)
    return shard


def bilinear(frac_rows, frac_cols):
    return (
        (1.0 - frac_rows) * (1.0 - frac_cols),
        (1.0 - frac_rows) * frac_cols,
        frac_rows * (1.0 - frac_cols),
        frac_rows * frac_cols,
    )


def fold_rows(buffer, rim_width, rows_dev):
    from_below = from_behind(buffer[:rim_width].astype(jnp.bfloat16), "row", -1).astype(jnp.float32)
    from_above = from_behind(buffer[rim_width + rows_dev :].astype(jnp.bfloat16), "row", 1).astype(
        jnp.float32
    )
    inner_rows = buffer[rim_width : rim_width + rows_dev]
    inner_rows = inner_rows.at[:rim_width].add(from_above)
    inner_rows = inner_rows.at[rows_dev - rim_width :].add(from_below)
    return inner_rows


def fold_cols(buffer, rim_width, cols_dev):
    from_right = from_behind(buffer[:, :rim_width].astype(jnp.bfloat16), "col", -1).astype(
        jnp.float32
    )
    from_left = from_behind(
        buffer[:, rim_width + cols_dev :].astype(jnp.bfloat16), "col", 1
    ).astype(jnp.float32)
    inner_cols = buffer[:, rim_width : rim_width + cols_dev]
    inner_cols = inner_cols.at[:, :rim_width].add(from_left)
    inner_cols = inner_cols.at[:, cols_dev - rim_width :].add(from_right)
    return inner_cols


def body(features, grad_out, weight, sample_taps, fraction, modulation):
    rows_dev, cols_dev, channels = features.shape
    tap_count = weight.shape[0]
    rim_width = BOUND + 1
    padded = with_halo(features, (("row", 0), ("col", 1)), rim_width)
    pad_rows = rows_dev + 2 * rim_width
    pad_cols = cols_dev + 2 * rim_width
    flat_feat = padded.reshape(pad_rows * pad_cols, channels)
    pixels = rows_dev * cols_dev
    first_row = lax.axis_index("row") * rows_dev - rim_width
    first_col = lax.axis_index("col") * cols_dev - rim_width
    local_rows = sample_taps[0].reshape(tap_count, pixels) - first_row
    local_cols = sample_taps[1].reshape(tap_count, pixels) - first_col
    anchors = local_rows * pad_cols + local_cols
    frac_rows = fraction[0].reshape(tap_count, pixels)
    frac_cols = fraction[1].reshape(tap_count, pixels)
    mask_flat = modulation.reshape(tap_count, pixels)
    grad_flat = grad_out.reshape(pixels, channels)
    gradient_sum = jnp.zeros((pad_rows * pad_cols, channels), jnp.float32)
    corner_steps = (0, 1, pad_cols, pad_cols + 1)
    columns = []
    for tap_index in range(tap_count):
        anchor = anchors[tap_index]
        mask_tap = mask_flat[tap_index]
        corners = bilinear(frac_rows[tap_index], frac_cols[tap_index])
        corner_ids = jnp.concatenate([anchor + step_size for step_size in corner_steps])
        gathered = jnp.take(flat_feat, corner_ids, axis=0).reshape(4, pixels, channels)
        sampled = jnp.zeros((pixels, channels), jnp.float32)
        for corner_index in range(4):
            sampled = sampled + corners[corner_index][:, None] * gathered[corner_index].astype(
                jnp.float32
            )
        columns.append((mask_tap[:, None] * sampled).astype(jnp.bfloat16))
        grad_cols = lax.dot_general(
            grad_flat,
            weight[tap_index],
            (((1,), (1,)), ((), ())),
            preferred_element_type=jnp.float32,
        )
        corner_mass = mask_tap[None, :] * jnp.stack(corners)
        updates = (corner_mass[:, :, None] * grad_cols[None]).reshape(4 * pixels, channels)
        gradient_sum = gradient_sum.at[corner_ids].add(updates)
    im2col = jnp.concatenate(columns, axis=1)
    grad_scale = 1.0 / math.sqrt(
        float(lax.axis_size("row") * rows_dev * lax.axis_size("col") * cols_dev)
    )
    partial_sums = lax.psum_scatter(
        lax.dot_general(
            im2col, grad_flat, (((0,), (0,)), ((), ())), preferred_element_type=jnp.float32
        ),
        "row",
        scatter_dimension=0,
        tiled=True,
    )
    reduced = lax.psum_scatter(partial_sums, "col", scatter_dimension=1, tiled=True)
    grad_w = reduced.T * grad_scale
    grid_sum = gradient_sum.reshape(pad_rows, pad_cols, channels)
    folded = fold_cols(fold_rows(grid_sum, rim_width, rows_dev), rim_width, cols_dev)
    grad_x = folded.astype(jnp.bfloat16)
    return (grad_x, grad_w)


def solution(mesh):
    in_specs = (
        P("row", "col", None),
        P("row", "col", None),
        P(),
        P(None, None, "row", "col"),
        P(None, None, "row", "col"),
        P(None, "row", "col"),
    )
    out_specs = (P("row", "col", None), P("col", "row"))
    return jax.shard_map(body, mesh=mesh, in_specs=in_specs, out_specs=out_specs, check_vma=False)
```

profile of v0, /device:TPU:1, one launch (start us, length us, event | category | flops | bytes accessed | tf_op | source)
XLA Modules:
  0.0 604.5 jit_solution(13449318150607254841)
XLA Ops:
  8.7 4.9 collective-permute-start.4
  13.7 1.9 collective-permute-start.5
  30.8 2.1 fusion.26
  36.2 2.1 fusion.24
  41.6 2.1 fusion.22
  47.1 2.1 fusion.20
  52.7 2.1 fusion.18
  57.5 2.1 fusion.16
  60.6 2.1 fusion.14
  95.1 2.1 fusion.12
  97.8 3.1 collective-permute-start.6
  102.5 9.1 %collective-permute-done.6 = bf16[58,17,256]{2,0,1:T(8,128)(2,1)S(1)} collective-permute-done((bf16[58,17,256]{2,0,1:T(8,128)(2,1)S(1)}, bf16[58,17,256]{2,0,1:T(8,128)(2,1)S(1)}, u32[]{:S(2)}, u32[]{:S(2)}) %collective-permute-start.6) | collective-permute-done | bytes 504864 | tf_op jit(solution)/shard_map/ppermute | solution.py:24
  111.5 4.1 collective-permute-done.7
  116.3 2.5 copy.13
  118.8 2.6 reshape.3040
  121.4 13.0 %gather_fusion = bf16[3072,256]{1,0:T(8,128)(2,1)} fusion(bf16[3828,256]{1,0:T(8,128)(2,1)S(1)} %reshape.3040, s32[3072]{0:T(1024)S(1)} %copy-done.89), kind=kCustom, calls=%fused_computation.clone | custom fusion | bytes 3158016 | tf_op jit(solution)/shard_map/jit(_take)/gather | solution.py:89
  134.4 13.0 %gather_fusion.1 = bf16[3072,256]{1,0:T(8,128)(2,1)} fusion(bf16[3828,256]{1,0:T(8,128)(2,1)S(1)} %reshape.3040, s32[3072]{0:T(1024)S(1)} %copy-done.91), kind=kCustom, calls=%fused_computation.1.clone | custom fusion | bytes 3158016 | tf_op jit(solution)/shard_map/jit(_take)/gather | solution.py:89
  147.5 13.0 %gather_fusion.2 = bf16[3072,256]{1,0:T(8,128)(2,1)} fusion(bf16[3828,256]{1,0:T(8,128)(2,1)S(1)} %reshape.3040, s32[3072]{0:T(1024)S(1)} %copy-done.90), kind=kCustom, calls=%fused_computation.2.clone | custom fusion | bytes 3158016 | tf_op jit(solution)/shard_map/jit(_take)/gather | solution.py:89
  160.5 13.0 %gather_fusion.3 = bf16[3072,256]{1,0:T(8,128)(2,1)} fusion(bf16[3828,256]{1,0:T(8,128)(2,1)S(1)} %reshape.3040, s32[3072]{0:T(1024)S(1)} %copy-done.93), kind=kCustom, calls=%fused_computation.3.clone | custom fusion | bytes 3158016 | tf_op jit(solution)/shard_map/jit(_take)/gather | solution.py:89
  173.6 13.0 %gather_fusion.4 = bf16[3072,256]{1,0:T(8,128)(2,1)} fusion(bf16[3828,256]{1,0:T(8,128)(2,1)S(1)} %reshape.3040, s32[3072]{0:T(1024)S(1)} %copy-done.92), kind=kCustom, calls=%fused_computation.4.clone | custom fusion | bytes 3158016 | tf_op jit(solution)/shard_map/jit(_take)/gather | solution.py:89
  186.6 13.0 %gather_fusion.5 = bf16[3072,256]{1,0:T(8,128)(2,1)} fusion(bf16[3828,256]{1,0:T(8,128)(2,1)S(1)} %reshape.3040, s32[3072]{0:T(1024)S(1)} %copy-done.95), kind=kCustom, calls=%fused_computation.5.clone | custom fusion | bytes 3158016 | tf_op jit(solution)/shard_map/jit(_take)/gather | solution.py:89
  199.6 13.0 %gather_fusion.6 = bf16[3072,256]{1,0:T(8,128)(2,1)} fusion(bf16[3828,256]{1,0:T(8,128)(2,1)S(1)} %reshape.3040, s32[3072]{0:T(1024)S(1)} %copy-done.94), kind=kCustom, calls=%fused_computation.6.clone | custom fusion | bytes 3158016 | tf_op jit(solution)/shard_map/jit(_take)/gather | solution.py:89
  212.7 13.0 %gather_fusion.7 = bf16[3072,256]{1,0:T(8,128)(2,1)} fusion(bf16[3828,256]{1,0:T(8,128)(2,1)S(1)} %reshape.3040, s32[3072]{0:T(1024)S(1)} %copy-done.97), kind=kCustom, calls=%fused_computation.7.clone | custom fusion | bytes 3158016 | tf_op jit(solution)/shard_map/jit(_take)/gather | solution.py:89
  225.7 13.0 %gather_fusion.8 = bf16[3072,256]{1,0:T(8,128)(2,1)} fusion(bf16[3828,256]{1,0:T(8,128)(2,1)S(1)} %reshape.3040, s32[3072]{0:T(1024)S(1)} %copy-done.96), kind=kCustom, calls=%fused_computation.8.clone | custom fusion | bytes 3158016 | tf_op jit(solution)/shard_map/jit(_take)/gather | solution.py:89
  238.8 2.8 broadcast_select_fusion.8
  241.7 1.6 broadcast_select_fusion.7
  243.3 1.6 broadcast_select_fusion.6
  244.9 1.6 broadcast_select_fusion.5
  246.6 1.6 broadcast_select_fusion.4
  248.2 1.6 broadcast_select_fusion.3
  249.9 1.6 broadcast_select_fusion.2
  251.5 1.8 broadcast_select_fusion.1
  253.4 1.6 broadcast_select_fusion
  263.3 2.5 fusion.46
  266.7 2.1 bitcast_multiply_fusion.8
  268.9 1.7 bitcast_multiply_fusion.7
  270.7 2.1 bitcast_multiply_fusion.6
  272.8 2.1 bitcast_multiply_fusion.5
  275.0 2.2 bitcast_multiply_fusion.4
  277.2 2.2 bitcast_multiply_fusion.3
  279.4 2.2 bitcast_multiply_fusion.2
  281.7 2.2 bitcast_multiply_fusion.1
  283.9 2.2 bitcast_multiply_fusion
  286.1 20.0 %scatter_custom_fusion = f32[3828,256]{1,0:T(8,128)} fusion(s32[3072]{0:T(1024)} %bitcast.234, f32[3072,256]{1,0:T(8,128)} %bitcast_multiply_fusion.8, f32[]{:T(128)} %constant.135.clone.1), kind=kCustom, calls=%fused_computation.28 | custom fusion | flops 786432 | bytes 3920384 | tf_op jit(solution)/shard_map/scatter-add | solution.py:104
  306.1 21.1 %scatter_fusion = f32[3828,256]{1,0:T(8,128)} fusion(f32[3828,256]{1,0:T(8,128)} %scatter_custom_fusion, s32[3072]{0:T(1024)S(1)} %bitcast.207, f32[3072,256]{1,0:T(8,128)S(1)} %bitcast_multiply_fusion.7), kind=kCustom, calls=%fused_computation.10 | custom fusion | flops 786432 | bytes 9449472 | tf_op jit(solution)/shard_map/scatter-add | solution.py:104
  327.1 21.5 %scatter_fusion.1 = f32[3828,256]{1,0:T(8,128)} fusion(f32[3828,256]{1,0:T(8,128)} %scatter_fusion, s32[3072]{0:T(1024)S(1)} %bitcast.208, f32[3072,256]{1,0:T(8,128)} %bitcast_multiply_fusion.6), kind=kCustom, calls=%fused_computation.11 | custom fusion | flops 786432 | bytes 9449472 | tf_op jit(solution)/shard_map/scatter-add | solution.py:104
  348.7 21.1 %scatter_fusion.2 = f32[3828,256]{1,0:T(8,128)} fusion(f32[3828,256]{1,0:T(8,128)} %scatter_fusion.1, s32[3072]{0:T(1024)S(1)} %bitcast.209, f32[3072,256]{1,0:T(8,128)S(1)} %copy-done.3), kind=kCustom, calls=%fused_computation.12 | custom fusion | flops 786432 | bytes 9449472 | tf_op jit(solution)/shard_map/scatter-add | solution.py:104
  369.7 21.7 %scatter_fusion.3 = f32[3828,256]{1,0:T(8,128)} fusion(f32[3828,256]{1,0:T(8,128)} %scatter_fusion.2, s32[3072]{0:T(1024)S(1)} %bitcast.210, f32[3072,256]{1,0:T(8,128)} %bitcast_multiply_fusion.4), kind=kCustom, calls=%fused_computation.13 | custom fusion | flops 786432 | bytes 9449472 | tf_op jit(solution)/shard_map/scatter-add | solution.py:104
  391.5 21.0 %scatter_fusion.4 = f32[3828,256]{1,0:T(8,128)} fusion(f32[3828,256]{1,0:T(8,128)} %scatter_fusion.3, s32[3072]{0:T(1024)S(1)} %bitcast.211, f32[3072,256]{1,0:T(8,128)S(1)} %copy-done.4), kind=kCustom, calls=%fused_computation.14 | custom fusion | flops 786432 | bytes 9449472 | tf_op jit(solution)/shard_map/scatter-add | solution.py:104
  412.5 21.4 %scatter_fusion.5 = f32[3828,256]{1,0:T(8,128)} fusion(f32[3828,256]{1,0:T(8,128)} %scatter_fusion.4, s32[3072]{0:T(1024)S(1)} %bitcast.212, f32[3072,256]{1,0:T(8,128)} %bitcast_multiply_fusion.2), kind=kCustom, calls=%fused_computation.15 | custom fusion | flops 786432 | bytes 9449472 | tf_op jit(solution)/shard_map/scatter-add | solution.py:104
  434.0 21.5 %scatter_fusion.6 = f32[3828,256]{1,0:T(8,128)} fusion(f32[3828,256]{1,0:T(8,128)} %scatter_fusion.5, s32[3072]{0:T(1024)S(1)} %bitcast.213, f32[3072,256]{1,0:T(8,128)} %bitcast_multiply_fusion.1), kind=kCustom, calls=%fused_computation.16 | custom fusion | flops 786432 | bytes 9449472 | tf_op jit(solution)/shard_map/scatter-add | solution.py:104
  455.7 21.2 %scatter_fusion.7 = f32[3828,256]{1,0:T(8,128)} fusion(f32[3828,256]{1,0:T(8,128)} %scatter_fusion.6, s32[3072]{0:T(1024)S(1)} %bitcast.214, f32[3072,256]{1,0:T(8,128)S(1)} %copy-done.2), kind=kCustom, calls=%fused_computation.17 | custom fusion | flops 786432 | bytes 9449472 | tf_op jit(solution)/shard_map/scatter-add | solution.py:104
  476.9 2.3 convert.8
  480.3 5.7 collective-permute-start
  487.0 1.9 collective-permute-start.1
  488.9 2.8 slice.604
  491.7 2.4 slice.605
  494.1 1.5 slice.527
  501.1 3.1 collective-permute-start.2
  505.6 2.2 collective-permute-done.2
  507.9 4.6 scatter-add.94
  512.6 1.6 copy.15
  515.3 3.8 scatter-add.95
  519.9 76.0 %reduce-scatter.7.cloned.1.call-done = f32[32,72]{1,0:T(8,128)} async-done(((f32[256,72]{1,0:T(8,128)}), f32[32,72]{1,0:T(8,128)}) %reduce-scatter.7.cloned.1.call-update) | async-done | bytes 9232
  (576 shorter events, 89.6 us)
Async XLA Ops:
  7.2 22.4 %copy-start = (bf16[24,32,256]{2,1,0:T(8,128)(2,1)S(1)}, bf16[24,32,256]{2,1,0:T(8,128)(2,1)}, u32[]{:S(2)}) copy-start(bf16[24,32,256]{2,1,0:T(8,128)(2,1)} %param.17) | copy-start | bytes 1179652
  7.2 18.1 %copy-start.20 = (f32[2,9,24,32]{3,2,1,0:T(8,128)S(1)}, f32[2,9,24,32]{3,2,1,0:T(8,128)}, u32[]{:S(2)}) copy-start(f32[2,9,24,32]{3,2,1,0:T(8,128)} %param.20) | copy-start | bytes 165892
  7.2 505.4 %reduce-scatter.5.cloned.1.call-start = ((), (), s32[]{:S(2)}) async-start(), calls=%async_computation.2 | async-start | bytes 2433024 | tf_op jit(solution)/shard_map/reduce_scatter | solution.py:109
  8.7 88.5 %collective-permute-start.4 = (bf16[17,32,256]{2,0,1:T(8,128)(2,1)S(1)}, bf16[17,32,256]{2,0,1:T(8,128)(2,1)S(1)}, u32[]{:S(2)}, u32[]{:S(2)}) collective-permute-start(bf16[17,32,256]{2,0,1:T(8,128)(2,1)S(1)} %get-tuple-element.63), channel_id=1, source_target_pairs={{0,8},{8,16},{16,24},{24,32},{32,40},{40,48},{48,56},{56,64},{64,7... | collective-permute-start | bytes 835592 | tf_op jit(solution)/shard_map/ppermute | solution.py:24
  13.7 83.6 %collective-permute-start.5 = (bf16[17,32,256]{2,0,1:T(8,128)(2,1)S(1)}, bf16[17,32,256]{2,0,1:T(8,128)(2,1)S(1)}, u32[]{:S(2)}, u32[]{:S(2)}) collective-permute-start(bf16[17,32,256]{2,0,1:T(8,128)(2,1)S(1)} %get-tuple-element.64), channel_id=1, source_target_pairs={{8,0},{16,8},{24,16},{32,24},{40,32},{48,40},{56,48},{64,56},{72,6... | collective-permute-start | bytes 835592 | tf_op jit(solution)/shard_map/ppermute | solution.py:25
  25.3 13.0 %copy-start.36 = (s32[1,1,24,32]{3,2,1,0:T(8,128)S(1)}, s32[1,1,24,32]{3,2,1,0:T(8,128)}, u32[]{:S(2)}) copy-start(s32[1,1,24,32]{3,2,1,0:T(8,128)} %copy-done.35) | copy-start | bytes 9220
  30.8 13.0 %copy-start.34 = (s32[1,1,24,32]{3,2,1,0:T(8,128)S(1)}, s32[1,1,24,32]{3,2,1,0:T(8,128)}, u32[]{:S(2)}) copy-start(s32[1,1,24,32]{3,2,1,0:T(8,128)} %copy-done.33) | copy-start | bytes 9220
  32.9 16.3 %copy-start.32 = (s32[1,1,24,32]{3,2,1,0:T(8,128)S(1)}, s32[1,1,24,32]{3,2,1,0:T(8,128)}, u32[]{:S(2)}) copy-start(s32[1,1,24,32]{3,2,1,0:T(8,128)} %copy-done.31) | copy-start | bytes 9220
  38.3 16.5 %copy-start.30 = (s32[1,1,24,32]{3,2,1,0:T(8,128)S(1)}, s32[1,1,24,32]{3,2,1,0:T(8,128)}, u32[]{:S(2)}) copy-start(s32[1,1,24,32]{3,2,1,0:T(8,128)} %copy-done.29) | copy-start | bytes 9220
  43.7 15.9 %copy-start.28 = (s32[1,1,24,32]{3,2,1,0:T(8,128)S(1)}, s32[1,1,24,32]{3,2,1,0:T(8,128)}, u32[]{:S(2)}) copy-start(s32[1,1,24,32]{3,2,1,0:T(8,128)} %copy-done.27) | copy-start | bytes 9220
  49.2 13.8 %copy-start.22 = (f32[9,24,32]{2,1,0:T(8,128)S(1)}, f32[9,24,32]{2,1,0:T(8,128)}, u32[]{:S(2)}) copy-start(f32[9,24,32]{2,1,0:T(8,128)} %param.21) | copy-start | bytes 82948
  52.5 11.2 %copy-start.86 = (s32[768]{0:T(1024)S(1)}, s32[768]{0:T(1024)}, u32[]{:S(2)}) copy-start(s32[768]{0:T(1024)} %copy-done.85) | copy-start | bytes 9220
  52.5 11.2 %copy-start.84 = (s32[768]{0:T(1024)S(1)}, s32[768]{0:T(1024)}, u32[]{:S(2)}) copy-start(s32[768]{0:T(1024)} %copy-done.83) | copy-start | bytes 9220
  52.5 12.5 %copy-start.82 = (s32[768]{0:T(1024)S(1)}, s32[768]{0:T(1024)}, u32[]{:S(2)}) copy-start(s32[768]{0:T(1024)} %copy-done.81) | copy-start | bytes 9220
  52.5 12.5 %copy-start.80 = (s32[768]{0:T(1024)S(1)}, s32[768]{0:T(1024)}, u32[]{:S(2)}) copy-start(s32[768]{0:T(1024)} %copy-done.79) | copy-start | bytes 9220
  52.5 12.5 %copy-start.78 = (s32[768]{0:T(1024)S(1)}, s32[768]{0:T(1024)}, u32[]{:S(2)}) copy-start(s32[768]{0:T(1024)} %copy-done.77) | copy-start | bytes 9220
  52.5 13.8 %copy-start.64 = (s32[768]{0:T(1024)S(1)}, s32[768]{0:T(1024)}, u32[]{:S(2)}) copy-start(s32[768]{0:T(1024)} %copy-done.63) | copy-start | bytes 9220
  52.5 13.8 %copy-start.62 = (s32[768]{0:T(1024)S(1)}, s32[768]{0:T(1024)}, u32[]{:S(2)}) copy-start(s32[768]{0:T(1024)} %copy-done.61) | copy-start | bytes 9220
  52.5 13.8 %copy-start.60 = (s32[768]{0:T(1024)S(1)}, s32[768]{0:T(1024)}, u32[]{:S(2)}) copy-start(s32[768]{0:T(1024)} %copy-done.59) | copy-start | bytes 9220
  52.6 15.1 %copy-start.76 = (s32[768]{0:T(1024)S(1)}, s32[768]{0:T(1024)}, u32[]{:S(2)}) copy-start(s32[768]{0:T(1024)} %copy-done.75) | copy-start | bytes 9220
  52.6 15.1 %copy-start.74 = (s32[768]{0:T(1024)S(1)}, s32[768]{0:T(1024)}, u32[]{:S(2)}) copy-start(s32[768]{0:T(1024)} %copy-done.73) | copy-start | bytes 9220
  52.6 15.1 %copy-start.72 = (s32[768]{0:T(1024)S(1)}, s32[768]{0:T(1024)}, u32[]{:S(2)}) copy-start(s32[768]{0:T(1024)} %copy-done.71) | copy-start | bytes 9220
  52.6 16.4 %copy-start.58 = (s32[768]{0:T(1024)S(1)}, s32[768]{0:T(1024)}, u32[]{:S(2)}) copy-start(s32[768]{0:T(1024)} %copy-done.57) | copy-start | bytes 9220
  52.6 16.4 %copy-start.56 = (s32[768]{0:T(1024)S(1)}, s32[768]{0:T(1024)}, u32[]{:S(2)}) copy-start(s32[768]{0:T(1024)} %copy-done.55) | copy-start | bytes 9220
  52.6 16.4 %copy-start.54 = (s32[768]{0:T(1024)S(1)}, s32[768]{0:T(1024)}, u32[]{:S(2)}) copy-start(s32[768]{0:T(1024)} %copy-done.53) | copy-start | bytes 9220
  52.6 17.7 %copy-start.70 = (s32[768]{0:T(1024)S(1)}, s32[768]{0:T(1024)}, u32[]{:S(2)}) copy-start(s32[768]{0:T(1024)} %copy-done.69) | copy-start | bytes 9220
  52.6 17.7 %copy-start.68 = (s32[768]{0:T(1024)S(1)}, s32[768]{0:T(1024)}, u32[]{:S(2)}) copy-start(s32[768]{0:T(1024)} %copy-done.67) | copy-start | bytes 9220
  52.6 17.7 %copy-start.66 = (s32[768]{0:T(1024)S(1)}, s32[768]{0:T(1024)}, u32[]{:S(2)}) copy-start(s32[768]{0:T(1024)} %copy-done.65) | copy-start | bytes 9220
  52.6 19.0 %copy-start.52 = (s32[768]{0:T(1024)S(1)}, s32[768]{0:T(1024)}, u32[]{:S(2)}) copy-start(s32[768]{0:T(1024)} %copy-done.51) | copy-start | bytes 9220
  56.8 22.0 %copy-start.161 = (f32[768]{0:T(1024)S(1)}, f32[768]{0:T(1024)}, u32[]{:S(2)}) copy-start(f32[768]{0:T(1024)} %squeeze.228) | copy-start | bytes 9220
  57.5 27.3 %copy-start.175 = (f32[1,768,1]{1,2,0:T(1,128)S(1)}, f32[1,768,1]{1,2,0:T(1,128)}, u32[]{:S(2)}) copy-start(f32[1,768,1]{1,2,0:T(1,128)} %squeeze.205) | copy-start | bytes 9220
  57.5 27.4 %copy-start.176 = (f32[1,768,1]{1,2,0:T(1,128)S(1)}, f32[1,768,1]{1,2,0:T(1,128)}, u32[]{:S(2)}) copy-start(f32[1,768,1]{1,2,0:T(1,128)} %squeeze.206) | copy-start | bytes 9220
  95.1 166.5 %copy-start.111 = (f32[768]{0:T(1024)}, f32[768]{0:T(1024)S(1)}, u32[]{:S(2)}) copy-start(f32[768]{0:T(1024)S(1)} %mul.1442) | copy-start | bytes 9220
  97.8 13.7 %collective-permute-start.6 = (bf16[58,17,256]{2,0,1:T(8,128)(2,1)S(1)}, bf16[58,17,256]{2,0,1:T(8,128)(2,1)S(1)}, u32[]{:S(2)}, u32[]{:S(2)}) collective-permute-start(bf16[58,17,256]{2,0,1:T(8,128)(2,1)S(1)} %get-tuple-element.59), channel_id=1, source_target_pairs={{0,1},{1,2},{2,3},{3,4},{4,5},{5,6},{6,7},{8,9},{9,10},{10,11},{11... | collective-permute-start | bytes 1514504 | tf_op jit(solution)/shard_map/ppermute | solution.py:24
  101.0 14.7 %collective-permute-start.7 = (bf16[58,17,256]{2,0,1:T(8,128)(2,1)S(1)}, bf16[58,17,256]{2,0,1:T(8,128)(2,1)S(1)}, u32[]{:S(2)}, u32[]{:S(2)}) collective-permute-start(bf16[58,17,256]{2,0,1:T(8,128)(2,1)S(1)} %get-tuple-element.60), channel_id=1, source_target_pairs={{1,0},{2,1},{3,2},{4,3},{5,4},{6,5},{7,6},{9,8},{10,9},{11,10},{12... | collective-permute-start | bytes 1514504 | tf_op jit(solution)/shard_map/ppermute | solution.py:25
  121.4 13.0 %copy-start.91 = (s32[3072]{0:T(1024)S(1)}, s32[3072]{0:T(1024)}, u32[]{:S(2)}) copy-start(s32[3072]{0:T(1024)} %get-tuple-element.207) | copy-start | bytes 36868
  134.4 13.0 %copy-start.90 = (s32[3072]{0:T(1024)S(1)}, s32[3072]{0:T(1024)}, u32[]{:S(2)}) copy-start(s32[3072]{0:T(1024)} %get-tuple-element.206) | copy-start | bytes 36868
  147.5 13.0 %copy-start.93 = (s32[3072]{0:T(1024)S(1)}, s32[3072]{0:T(1024)}, u32[]{:S(2)}) copy-start(s32[3072]{0:T(1024)} %get-tuple-element.205) | copy-start | bytes 36868
  160.5 13.1 %copy-start.92 = (s32[3072]{0:T(1024)S(1)}, s32[3072]{0:T(1024)}, u32[]{:S(2)}) copy-start(s32[3072]{0:T(1024)} %get-tuple-element.204) | copy-start | bytes 36868
  173.6 13.0 %copy-start.95 = (s32[3072]{0:T(1024)S(1)}, s32[3072]{0:T(1024)}, u32[]{:S(2)}) copy-start(s32[3072]{0:T(1024)} %get-tuple-element.203) | copy-start | bytes 36868
  186.6 13.0 %copy-start.94 = (s32[3072]{0:T(1024)S(1)}, s32[3072]{0:T(1024)}, u32[]{:S(2)}) copy-start(s32[3072]{0:T(1024)} %get-tuple-element.202) | copy-start | bytes 36868
  199.6 13.0 %copy-start.97 = (s32[3072]{0:T(1024)S(1)}, s32[3072]{0:T(1024)}, u32[]{:S(2)}) copy-start(s32[3072]{0:T(1024)} %get-tuple-element.201) | copy-start | bytes 36868
  212.7 13.0 %copy-start.96 = (s32[3072]{0:T(1024)S(1)}, s32[3072]{0:T(1024)}, u32[]{:S(2)}) copy-start(s32[3072]{0:T(1024)} %get-tuple-element.200) | copy-start | bytes 36868
  225.7 13.0 %copy-start.162 = (pred[3072]{0:T(1024)(128)(4,1)S(1)}, pred[3072]{0:T(1024)(128)(4,1)}, u32[]{:S(2)}) copy-start(pred[3072]{0:T(1024)(128)(4,1)} %compare_and_fusion.8) | copy-start | bytes 9220
  265.9 330.1 %reduce-scatter.7.cloned.1.call-start = ((), (), s32[]{:S(2)}) async-start(), calls=%async_computation.3 | async-start | bytes 147456
  286.1 20.0 %copy-start.98 = (s32[3072,1]{0,1:T(1,128)S(1)}, s32[3072,1]{0,1:T(1,128)}, u32[]{:S(2)}) copy-start(s32[3072,1]{0,1:T(1,128)} %compare_select_fusion.7) | copy-start | bytes 36868
  306.1 21.1 %copy-start.99 = (s32[3072,1]{0,1:T(1,128)S(1)}, s32[3072,1]{0,1:T(1,128)}, u32[]{:S(2)}) copy-start(s32[3072,1]{0,1:T(1,128)} %compare_select_fusion.6) | copy-start | bytes 36868
  327.1 21.6 %copy-start.3 = (f32[3072,256]{1,0:T(8,128)S(1)}, f32[3072,256]{1,0:T(8,128)}, u32[]{:S(2)}) copy-start(f32[3072,256]{1,0:T(8,128)} %bitcast_multiply_fusion.5) | copy-start | bytes 9437188
  327.1 21.6 %copy-start.100 = (s32[3072,1]{0,1:T(1,128)S(1)}, s32[3072,1]{0,1:T(1,128)}, u32[]{:S(2)}) copy-start(s32[3072,1]{0,1:T(1,128)} %compare_select_fusion.5) | copy-start | bytes 36868
  348.7 21.1 %copy-start.101 = (s32[3072,1]{0,1:T(1,128)S(1)}, s32[3072,1]{0,1:T(1,128)}, u32[]{:S(2)}) copy-start(s32[3072,1]{0,1:T(1,128)} %compare_select_fusion.4) | copy-start | bytes 36868
  369.7 21.7 %copy-start.4 = (f32[3072,256]{1,0:T(8,128)S(1)}, f32[3072,256]{1,0:T(8,128)}, u32[]{:S(2)}) copy-start(f32[3072,256]{1,0:T(8,128)} %bitcast_multiply_fusion.3) | copy-start | bytes 9437188
  369.7 21.7 %copy-start.102 = (s32[3072,1]{0,1:T(1,128)S(1)}, s32[3072,1]{0,1:T(1,128)}, u32[]{:S(2)}) copy-start(s32[3072,1]{0,1:T(1,128)} %compare_select_fusion.3) | copy-start | bytes 36868
  412.5 21.4 %copy-start.50 = (s32[768]{0:T(1024)S(1)}, s32[768]{0:T(1024)}, u32[]{:S(2)}) copy-start(s32[768]{0:T(1024)} %copy-done.49) | copy-start | bytes 9220
  412.5 21.4 %copy-start.48 = (s32[768]{0:T(1024)S(1)}, s32[768]{0:T(1024)}, u32[]{:S(2)}) copy-start(s32[768]{0:T(1024)} %copy-done.47) | copy-start | bytes 9220
  412.5 21.4 %copy-start.46 = (s32[768]{0:T(1024)S(1)}, s32[768]{0:T(1024)}, u32[]{:S(2)}) copy-start(s32[768]{0:T(1024)} %copy-done.45) | copy-start | bytes 9220
  434.0 21.6 %copy-start.44 = (s32[768]{0:T(1024)S(1)}, s32[768]{0:T(1024)}, u32[]{:S(2)}) copy-start(s32[768]{0:T(1024)} %copy-done.43) | copy-start | bytes 9220
  434.0 21.6 %copy-start.42 = (s32[768]{0:T(1024)S(1)}, s32[768]{0:T(1024)}, u32[]{:S(2)}) copy-start(s32[768]{0:T(1024)} %copy-done.41) | copy-start | bytes 9220
  434.0 21.6 %copy-start.40 = (s32[768]{0:T(1024)S(1)}, s32[768]{0:T(1024)}, u32[]{:S(2)}) copy-start(s32[768]{0:T(1024)} %copy-done.39) | copy-start | bytes 9220
  434.0 21.6 %copy-start.2 = (f32[3072,256]{1,0:T(8,128)S(1)}, f32[3072,256]{1,0:T(8,128)}, u32[]{:S(2)}) copy-start(f32[3072,256]{1,0:T(8,128)} %bitcast_multiply_fusion) | copy-start | bytes 9437188
  480.3 16.7 %collective-permute-start = (bf16[17,66,256]{2,1,0:T(8,128)(2,1)}, bf16[17,66,256]{2,1,0:T(8,128)(2,1)}, u32[]{:S(2)}, u32[]{:S(2)}) collective-permute-start(bf16[17,66,256]{2,1,0:T(8,128)(2,1)} %convert_element_type.160), channel_id=1, source_target_pairs={{0,8},{8,16},{16,24},{24,32},{32,40},{40,48},{48,56},{56,64},{64,7... | collective-permute-start | bytes 1723400 | tf_op jit(solution)/shard_map/ppermute | solution.py:14
  487.0 11.9 %collective-permute-start.1 = (bf16[17,66,256]{2,1,0:T(8,128)(2,1)}, bf16[17,66,256]{2,1,0:T(8,128)(2,1)}, u32[]{:S(2)}, u32[]{:S(2)}) collective-permute-start(bf16[17,66,256]{2,1,0:T(8,128)(2,1)} %convert_element_type.162), channel_id=1, source_target_pairs={{8,0},{16,8},{24,16},{32,24},{40,32},{48,40},{56,48},{64,56},{72,6... | collective-permute-start | bytes 1723400 | tf_op jit(solution)/shard_map/ppermute | solution.py:14
  501.1 6.7 %collective-permute-start.2 = (bf16[24,17,256]{2,1,0:T(8,128)(2,1)S(1)}, bf16[24,17,256]{2,1,0:T(8,128)(2,1)S(1)}, u32[]{:S(2)}, u32[]{:S(2)}) collective-permute-start(bf16[24,17,256]{2,1,0:T(8,128)(2,1)S(1)} %get-tuple-element.62), channel_id=1, source_target_pairs={{0,1},{1,2},{2,3},{3,4},{4,5},{5,6},{6,7},{8,9},{9,10},{10,11},{11... | collective-permute-start | bytes 626696 | tf_op jit(solution)/shard_map/ppermute | solution.py:14
  504.3 10.0 %collective-permute-start.3 = (bf16[24,17,256]{2,1,0:T(8,128)(2,1)}, bf16[24,17,256]{2,1,0:T(8,128)(2,1)}, u32[]{:S(2)}, u32[]{:S(2)}) collective-permute-start(bf16[24,17,256]{2,1,0:T(8,128)(2,1)} %get-tuple-element.61), channel_id=1, source_target_pairs={{1,0},{2,1},{3,2},{4,3},{5,4},{6,5},{7,6},{9,8},{10,9},{11,10},{12... | collective-permute-start | bytes 626696 | tf_op jit(solution)/shard_map/ppermute | solution.py:14
  507.9 89.5 %copy-start.1 = (bf16[24,32,256]{2,1,0:T(8,128)(2,1)S(1)}, bf16[24,32,256]{2,1,0:T(8,128)(2,1)}, u32[]{:S(2)}) copy-start(bf16[24,32,256]{2,1,0:T(8,128)(2,1)} %param.17) | copy-start | bytes 1179652
  (123 other events, 320.5 us)
Sparse Core Ops, SparseCore 0:
  266.0 121.3 reduce-scatter.4
  514.4 81.5 reduce-scatter.6
where the time goes:
time: 611 us; the launch traced here: 605 us
  other arithmetic  271 us (44%)
  local copies, waits for them, and re-layouts  180 us (29%)
  waiting for transfers between devices  92.2 us (15%)
  starting transfers between devices  23.5 us (4%)
  matrix products  20.5 us (3%)
  between operations  16.8 us (3%)
    scatter-add x9, other arithmetic, body(): gradient_sum = gradient_sum.at[corner_ids].add(updates)  191 us
    gather x9, local copies, waits for them, and re-layouts, body(): jnp.take(flat_feat, corner_ids, axis=0).reshape(4, pixels, channels)  117 us
    unnamed x3, waiting for transfers between devices  76 us
    mul x9, other arithmetic, body(): corner_mass[:, :, None] * grad_cols[None]  18.9 us
    dot_general x9, matrix products, body(): lax.dot_general(grad_flat, weight[tap_index], (((1,), (1,)), ((), ())), p...  18 us
    squeeze x36, local copies, waits for them, and re-layouts, body(): corners = bilinear(frac_rows[tap_index], frac_cols[tap_index])  16.8 us
    select_n x9, other arithmetic, body(): jnp.take(flat_feat, corner_ids, axis=0).reshape(4, pixels, channels)  15.8 us
    mul x18, other arithmetic, bilinear(): (1.0 - frac_rows) * (1.0 - frac_cols)  13.7 us
  transfers between devices with their start and end apart: 10, of which 5 were waited for; matrix products, arithmetic and copies ran while one was open for 53% of the time, Pallas kernels for 0%

commit v1 on v0

v1 whole, which is shorter than its diff:
```python
import functools
import math

import jax
import jax.numpy as jnp
from jax import lax
from jax.experimental import pallas as pl
from jax.experimental.pallas import tpu as pltpu
from jax.sharding import PartitionSpec as P

F32, BF16 = jnp.float32, jnp.bfloat16
MESH = pl.DeviceIdType.MESH
NN = (((1,), (0,)), ((), ()))
NT = (((1,), (1,)), ((), ()))

TAPS, CH = 9, 256
TR, TC = 24, 32
RIM = 17
WR, WC = TR + 2 * RIM, 64
STRIP = 8
REACH = STRIP + 2 * RIM
CHUNK = 6
NROW, NCOL = 32, 8
BLOCK = TAPS * CH // NROW
HALF = CH // NCOL // 2


def dot(a, b, dims=NN):
    return lax.dot_general(a, b, dims, preferred_element_type=F32)


def iota(shape, dim):
    return lax.broadcasted_iota(jnp.int32, shape, dim)


def mod(a, n):
    return lax.rem(a + n, n)


def kernel(
    aux, feat, gout, wgt,
    gx, gw,
    r_ref, c_ref, e_ref, gcol, gt,
    xbuf, ext, fwin, ft, fte,
    acc, acce, gsend, grecv, xf, csend, crecv,
    gbuf, rbuf, own, sbuf, cbuf, tbuf, dbuf,
    f_send, f_recv, g_send, g_recv, s1_send, s1_recv, s2_send, s2_recv, s3_send, s3_recv,
):
    me_r, me_c = lax.axis_index("row"), lax.axis_index("col")
    core = lax.rem(me_r, 2)
    up, down = mod(me_r - 1, NROW), mod(me_r + 1, NROW)
    left, right = mod(me_c - 1, NCOL), mod(me_c + 1, NCOL)
    sibling = me_r + 1 - 2 * core

    def remote(src, dst, send, recv, device):
        return pltpu.make_async_remote_copy(
            src_ref=src, dst_ref=dst, send_sem=send, recv_sem=recv, device_id=device, device_id_type=MESH
        )

    barrier = pltpu.get_barrier_semaphore()

    def greet_row(d, carry):
        pl.semaphore_signal(barrier, inc=1, device_id=(mod(me_r + d, NROW), me_c), device_id_type=MESH)
        return carry

    def greet_col(d, carry):
        pl.semaphore_signal(barrier, inc=1, device_id=(me_r, mod(me_c + d, NCOL)), device_id_type=MESH)
        return carry

    lax.fori_loop(1, NROW, greet_row, 0)
    lax.fori_loop(1, NCOL, greet_col, 0)

    row0 = (me_r * TR - RIM).astype(F32)
    col0 = (me_c * TC - 16).astype(F32)

    def hats(ks, carry):
        r = aux[0, pl.ds(ks, 1), :] - row0
        s = aux[1, pl.ds(ks, 1), :] - col0
        fy, fx = aux[2, pl.ds(ks, 1), :], aux[3, pl.ds(ks, 1), :]
        m = aux[4, pl.ds(ks, 1), :]
        ids = iota((64, 256), 0).astype(F32)
        r_ref[ks] = jnp.where(ids == r, m * (1.0 - fy), jnp.where(ids == r + 1.0, m * fy, 0.0))
        c_ref[ks] = jnp.where(ids == s, 1.0 - fx, jnp.where(ids == s + 1.0, fx, 0.0))
        e_ref[ks, pl.ds(0, 1)] = jnp.where(s == -1.0, 1.0 - fx, 0.0)
        e_ref[ks, pl.ds(1, 1)] = jnp.where(s == 63.0, fx, 0.0)
        return carry

    lax.fori_loop(0, 27, hats, 0)

    pick = iota((64, 768), 0)
    pick = TC * lax.rem(pick, 32) + 15 + lax.div(pick, 32)
    picked = (iota((64, 768), 1) == pick).astype(BF16)
    xbuf[...] = dot(picked, feat[...].reshape(768, CH)).astype(BF16).reshape(2, 32, CH)

    f_copies = [
        remote(feat.at[:, pl.ds(16, 16)], fwin.at[pl.ds(RIM, TR), pl.ds(0, 16)], f_send.at[0], f_recv.at[0], (me_r, right)),
        remote(feat.at[:, pl.ds(0, 16)], fwin.at[pl.ds(RIM, TR), pl.ds(48, 16)], f_send.at[1], f_recv.at[1], (me_r, left)),
        remote(xbuf.at[0], ext.at[0, 0], f_send.at[2], f_recv.at[2], (me_r, right)),
        remote(xbuf.at[1], ext.at[0, 1], f_send.at[3], f_recv.at[3], (me_r, left)),
        remote(feat.at[pl.ds(0, RIM)], fwin.at[pl.ds(RIM + TR, RIM), pl.ds(16, TC)], f_send.at[4], f_recv.at[4], (up, me_c)),
        remote(feat.at[pl.ds(TR - RIM, RIM)], fwin.at[pl.ds(0, RIM), pl.ds(16, TC)], f_send.at[5], f_recv.at[5], (down, me_c)),
        remote(fwin.at[pl.ds(RIM, RIM), pl.ds(0, 16)], fwin.at[pl.ds(RIM + TR, RIM), pl.ds(0, 16)], f_send.at[6], f_recv.at[6], (up, me_c)),
        remote(fwin.at[pl.ds(RIM, RIM), pl.ds(48, 16)], fwin.at[pl.ds(RIM + TR, RIM), pl.ds(48, 16)], f_send.at[7], f_recv.at[7], (up, me_c)),
        remote(fwin.at[pl.ds(TR, RIM), pl.ds(0, 16)], fwin.at[pl.ds(0, RIM), pl.ds(0, 16)], f_send.at[8], f_recv.at[8], (down, me_c)),
        remote(fwin.at[pl.ds(TR, RIM), pl.ds(48, 16)], fwin.at[pl.ds(0, RIM), pl.ds(48, 16)], f_send.at[9], f_recv.at[9], (down, me_c)),
        remote(ext.at[0], ext.at[2], f_send.at[10], f_recv.at[10], (up, me_c)),
        remote(ext.at[0], ext.at[1], f_send.at[11], f_recv.at[11], (down, me_c)),
    ]

    pl.semaphore_wait(barrier, NROW + NCOL - 2)
    for copy in f_copies[:6]:
        copy.start()
    fwin[RIM : RIM + TR, 16 : 16 + TC] = feat[...]

    def grad_cols(k, carry):
        gcol[k] = dot(gout[...], wgt[k], NT).astype(BF16)
        return carry

    lax.fori_loop(0, TAPS, grad_cols, 0)
    eye = (iota((CH, CH), 0) == iota((CH, CH), 1)).astype(BF16)
    gt[...] = dot(eye, gout[...], NT).astype(BF16)
    acc[...] = jnp.zeros_like(acc)
    acce[...] = jnp.zeros_like(acce)

    def block(ks, i0, n):
        c = c_ref[ks]
        return jnp.concatenate([(r_ref[ks, pl.ds(i0 + a, 1), :] * c).astype(BF16) for a in range(n)], axis=0)

    def edge(ks):
        r = r_ref[ks]
        return jnp.concatenate([(r * e_ref[ks, pl.ds(e, 1), :]).astype(BF16) for e in range(2)], axis=0)

    def scatter(s):
        rows = pl.ds(pl.multiple_of(256 * s, 256), 256)

        def step(q, carry):
            i0 = STRIP * s + q * CHUNK
            cells = pl.ds(pl.multiple_of(i0 * WC, WC), CHUNK * WC)
            total = acc[cells, :]
            for k in range(TAPS):
                total = total + dot(block(3 * k + s, i0, CHUNK), gcol[k, rows, :])
            acc[cells, :] = total
            return carry

        lax.fori_loop(0, REACH // CHUNK, step, 0)
        total = acce[...]
        for k in range(TAPS):
            total = total + dot(edge(3 * k + s), gcol[k, rows, :])
        acce[...] = total

    scatter(0)
    for copy in f_copies[:4]:
        copy.wait_recv()
    for copy in f_copies[6:]:
        copy.start()

    def rest(s, carry):
        scatter(s)
        return carry

    lax.fori_loop(1, 3, rest, 0)

    rim = RIM * WC
    gsend[0, :rim] = acc[:rim].astype(BF16)
    gsend[1, :rim] = acc[(RIM + TR) * WC :].astype(BF16)
    for e in range(2):
        gsend[0, rim + 32 * e : rim + 32 * e + 32] = acce[64 * e : 64 * e + 32].astype(BF16)
        gsend[1, rim + 32 * e : rim + 32 * e + 32] = acce[64 * e + 32 : 64 * e + 64].astype(BF16)
    g_copies = [
        remote(gsend.at[0], grecv.at[0], g_send.at[0], g_recv.at[0], (up, me_c)),
        remote(gsend.at[1], grecv.at[1], g_send.at[1], g_recv.at[1], (down, me_c)),
        remote(csend.at[0], crecv.at[0], g_send.at[2], g_recv.at[2], (me_r, left)),
        remote(csend.at[1], crecv.at[1], g_send.at[3], g_recv.at[3], (me_r, right)),
    ]
    g_copies[0].start()
    g_copies[1].start()

    for copy in f_copies[4:]:
        copy.wait_recv()

    def turn(q, carry):
        rows = fwin[pl.ds(2 * q, 2)].reshape(2 * WC, CH)
        ft[:, pl.ds(pl.multiple_of(q * 2 * WC, 2 * WC), 2 * WC)] = dot(eye, rows, NT).astype(BF16)
        return carry

    lax.fori_loop(0, WR // 2, turn, 0)
    at = iota((128, 192), 0)
    side, i = lax.div(at, 64), lax.rem(at, 64)
    slot = jnp.where(i < RIM, 64 + 7 + i, jnp.where(i < RIM + TR, i - RIM, 128 + i - RIM - TR)) + 32 * side
    chosen = ((iota((128, 192), 1) == slot) & (i < WR)).astype(BF16)
    edges = dot(chosen, ext[...].reshape(192, CH)).astype(BF16)
    fte[...] = dot(eye, edges, NT).astype(BF16)

    def sibling_copy(k):
        return remote(gbuf.at[k, 1 - core], rbuf.at[k], s1_send.at[k], s1_recv.at[k], (sibling, me_c))

    def col_copy(k, d):
        to = mod(me_c + d, NCOL)
        return remote(sbuf.at[k, to], cbuf.at[k, d - 1], s2_send.at[k, d - 1], s2_recv.at[k, d - 1], (me_r, to))

    def pass_on(k):
        sibling_copy(k).wait_recv()
        both = gbuf[k, core] + rbuf[k]
        rbuf[k] = both
        sbuf[k] = both.astype(BF16)

        def send(d, carry):
            col_copy(k, d).start()
            return carry

        lax.fori_loop(1, NCOL, send, 0)

    def fold_rows():
        g_copies[0].wait_recv()
        g_copies[1].wait_recv()
        span = pl.ds(TR * WC, rim)
        acc[span, :] = acc[span, :] + grecv[0, :rim].astype(F32)
        span = pl.ds(RIM * WC, rim)
        acc[span, :] = acc[span, :] + grecv[1, :rim].astype(F32)
        for e in range(2):
            xf[0] = grecv[0, rim + 32 * e : rim + 32 * e + 32].astype(F32)
            xf[1] = grecv[1, rim + 32 * e : rim + 32 * e + 32].astype(F32)
            span = pl.ds(64 * e + TR, RIM)
            acce[span, :] = acce[span, :] + xf[0, pl.ds(0, RIM)]
            span = pl.ds(64 * e + RIM, RIM)
            acce[span, :] = acce[span, :] + xf[1, pl.ds(9, RIM)]
        own_rows = acc[RIM * WC : (RIM + TR) * WC].reshape(TR, WC, CH)
        for e in range(2):
            csend[e, : TR * 16] = own_rows[:, 48 * e : 48 * e + 16].astype(BF16).reshape(TR * 16, CH)
            csend[e, TR * 16 :] = acce[pl.ds(64 * e + RIM, 32), :].astype(BF16)
        g_copies[2].start()
        g_copies[3].start()

    def tap(k, carry):
        total_w = None
        for s in range(3):
            ks = 3 * k + s
            total = None
            for q in range(11):
                at = STRIP * WC * s + 256 * q
                if q < 10:
                    lhs, rhs = ft[:, at : at + 256], block(ks, STRIP * s + 4 * q, 4)
                else:
                    lhs = jnp.concatenate([ft[:, at : at + 128], fte[...]], axis=1)
                    rhs = jnp.concatenate([block(ks, STRIP * s + 40, 2), edge(ks)], axis=0)
                part = dot(lhs, rhs)
                total = part if total is None else total + part
            part = dot(gt[:, 256 * s : 256 * s + 256], total.astype(BF16), NT)
            total_w = part if total_w is None else total_w + part
        cut = total_w.reshape(NCOL, 2, HALF, CH)
        gbuf[k, 0] = cut[:, 0]
        gbuf[k, 1] = cut[:, 1]
        sibling_copy(k).start()

        @pl.when(k > 0)
        def _():
            pass_on(k - 1)

        @pl.when(k == 4)
        def _():
            fold_rows()

        return carry

    lax.fori_loop(0, TAPS, tap, 0)
    pass_on(TAPS - 1)

    g_copies[2].wait_recv()
    g_copies[3].wait_recv()
    xf[0] = crecv[0, TR * 16 :].astype(F32)
    xf[1] = crecv[1, TR * 16 :].astype(F32)
    column = iota((TC, CH), 0)

    def finish(i, carry):
        row = acc[pl.ds(pl.multiple_of((RIM + i) * WC + 16, 16), TC), :]
        span = pl.ds(pl.multiple_of(i * 16, 16), 16)
        row = row + jnp.concatenate([crecv[1, span, :], crecv[0, span, :]], axis=0).astype(F32)
        row = row + jnp.where(column == 15, xf[0, pl.ds(i, 1), :], jnp.where(column == 16, xf[1, pl.ds(i, 1), :], 0.0))
        gx[i] = row.astype(BF16)
        return carry

    lax.fori_loop(0, TR, finish, 0)

    def gather_cols(k, carry):
        total = rbuf[k, me_c]
        for d in range(1, NCOL):
            col_copy(k, d).wait_recv()
            total = total + cbuf[k, d - 1].astype(F32)
        own[k] = total
        return carry

    lax.fori_loop(0, TAPS, gather_cols, 0)
    flat = jnp.concatenate([own[k] for k in range(TAPS)] + [jnp.zeros((HALF, 128), F32)], axis=1)
    for b in range(NROW):
        tbuf[b] = flat[:, BLOCK * b : BLOCK * b + 128].astype(BF16)

    def row_copy(d):
        to = mod(me_r + d, NROW)
        return remote(tbuf.at[to], dbuf.at[d - 1], s3_send.at[d - 1], s3_recv.at[d - 1], (to, me_c))

    def send_row(d, carry):
        row_copy(d).start()
        return carry

    lax.fori_loop(1, NROW, send_row, 0)

    def gather_rows(d, carry):
        row_copy(d).wait_recv()
        same, other = carry
        piece = dbuf[d - 1].astype(F32)
        odd = lax.rem(d, 2) == 1
        return jnp.where(odd, same, same + piece), jnp.where(odd, other + piece, other)

    same, other = lax.fori_loop(
        1, NROW, gather_rows, (tbuf[me_r].astype(F32), jnp.zeros((HALF, 128), F32))
    )
    scale = 1.0 / math.sqrt(float(NROW * TR * NCOL * TC))
    gw[0:HALF] = jnp.where(core == 0, same, other)[:, :BLOCK] * scale
    gw[HALF : 2 * HALF] = jnp.where(core == 0, other, same)[:, :BLOCK] * scale

    for copy in f_copies + g_copies:
        copy.wait_send()

    def drain(k, carry):
        sibling_copy(k).wait_send()
        for d in range(1, NCOL):
            col_copy(k, d).wait_send()
        return carry

    lax.fori_loop(0, TAPS, drain, 0)

    def drain_row(d, carry):
        row_copy(d).wait_send()
        return carry

    lax.fori_loop(1, NROW, drain_row, 0)


def body(features, grad_out, weight, sample_taps, fraction, modulation):
    aux = jnp.concatenate([sample_taps.astype(F32), fraction, modulation[None]], axis=0)
    aux = aux.reshape(5, 27, 256)
    vmem = pl.BlockSpec(memory_space=pltpu.VMEM)
    dma = pltpu.SemaphoreType.DMA
    return pl.pallas_call(
        kernel,
        name="deform_backward",
        out_shape=(
            jax.ShapeDtypeStruct((TR, TC, CH), BF16),
            jax.ShapeDtypeStruct((2 * HALF, BLOCK), F32),
        ),
        in_specs=[vmem] * 4,
        out_specs=(vmem, vmem),
        scratch_shapes=[
            pltpu.VMEM((27, 64, 256), F32),
            pltpu.VMEM((27, 64, 256), F32),
            pltpu.VMEM((27, 8, 256), F32),
            pltpu.VMEM((TAPS, 768, CH), BF16),
            pltpu.VMEM((CH, 768), BF16),
            pltpu.VMEM((2, 32, CH), BF16),
            pltpu.VMEM((3, 2, 32, CH), BF16),
            pltpu.VMEM((WR, WC, CH), BF16),
            pltpu.VMEM((CH, WR * WC), BF16),
            pltpu.VMEM((CH, 128), BF16),
            pltpu.VMEM((WR * WC, CH), F32),
            pltpu.VMEM((128, CH), F32),
            pltpu.VMEM((2, RIM * WC + 64, CH), BF16),
            pltpu.VMEM((2, RIM * WC + 64, CH), BF16),
            pltpu.VMEM((2, 32, CH), F32),
            pltpu.VMEM((2, TR * 16 + 32, CH), BF16),
            pltpu.VMEM((2, TR * 16 + 32, CH), BF16),
            pltpu.VMEM((TAPS, 2, NCOL, HALF, CH), F32),
            pltpu.VMEM((TAPS, NCOL, HALF, CH), F32),
            pltpu.VMEM((TAPS, HALF, CH), F32),
            pltpu.VMEM((TAPS, NCOL, HALF, CH), BF16),
            pltpu.VMEM((TAPS, NCOL - 1, HALF, CH), BF16),
            pltpu.VMEM((NROW, HALF, 128), BF16),
            pltpu.VMEM((NROW - 1, HALF, 128), BF16),
            dma((12,)), dma((12,)), dma((4,)), dma((4,)),
            dma((TAPS,)), dma((TAPS,)), dma((TAPS, NCOL - 1)), dma((TAPS, NCOL - 1)),
            dma((NROW - 1,)), dma((NROW - 1,)),
        ],
        compiler_params=pltpu.CompilerParams(
            collective_id=0, has_side_effects=True, vmem_limit_bytes=56 * 2**20
        ),
        cost_estimate=pl.CostEstimate(flops=22 * 10**9, bytes_accessed=8 * 10**6, transcendentals=0),
    )(aux, features, grad_out.reshape(768, CH), weight)


def solution(mesh):
    in_specs = (
        P("row", "col", None),
        P("row", "col", None),
        P(),
        P(None, None, "row", "col"),
        P(None, None, "row", "col"),
        P(None, "row", "col"),
    )
    out_specs = (P("row", "col", None), P("col", "row"))
    return jax.shard_map(body, mesh=mesh, in_specs=in_specs, out_specs=out_specs, check_vma=False)
```

time: 611 us -> 75 us (0.12); the launches traced: 605 us -> 74.7 us
  other arithmetic: 271 us -> 1.63 us
  local copies, waits for them, and re-layouts: 180 us -> 5.25 us
  waiting for transfers between devices: 92.2 us -> 0 us
  Pallas kernels: 0 us -> 67.2 us
  starting transfers between devices: 23.5 us -> 0 us
  matrix products: 20.5 us -> 0 us
  between operations: 16.8 us -> 0.65 us
    scatter-add x11 -> x0, other arithmetic: 193 us -> none  [the longest x9 191 us: body(): gradient_sum = gradient_sum.at[corner_ids].add(updates)]
    gather x9 -> x0, local copies, waits for them, and re-layouts: 117 us -> none  [body(): jnp.take(flat_feat, corner_ids, axis=0).reshape(4, pixels, channels)]
    unnamed x3 -> x0, waiting for transfers between devices: 76 us -> none
    pallas_call x0 -> x1, Pallas kernels: none -> 67.2 us  [body(): pl.pallas_call(kernel, name='deform_backward', out_shape=(jax.ShapeDtypeS...]
    mul x37 -> x0, other arithmetic: 32.7 us -> none  [the longest x9 18.9 us: body(): corner_mass[:, :, None] * grad_cols[None]]
    ppermute x8 -> x0, starting transfers between devices: 23.4 us -> none  [the longest x4 12 us: from_behind(): return lax.ppermute(shard, axis, pairs)]
    dot_general x10 -> x0, matrix products: 20.5 us -> none  [the longest x9 18 us: body(): lax.dot_general(grad_flat, weight[tap_index], (((1,), (1,)), ((), ())), p...]
    select_n x18 -> x0, other arithmetic: 19.5 us -> none  [the longest x9 15.8 us: body(): jnp.take(flat_feat, corner_ids, axis=0).reshape(4, pixels, channels)]
  transfers between devices with their start and end apart: 10 -> 0, of which waited for: 5 -> 0; matrix products, arithmetic and copies ran while one was open for 53% -> 0% of each run, Pallas kernels for 0% -> 0%
where the time goes in v1:
time: 75 us; the launch traced here: 74.7 us
  Pallas kernels  67.2 us (90%)
  local copies, waits for them, and re-layouts  5.25 us (7%)
  other arithmetic  1.63 us (2%)
    pallas_call x1, Pallas kernels, body(): pl.pallas_call(kernel, name='deform_backward', out_shape=(jax.ShapeDtypeS...  67.2 us
    unnamed x2, local copies, waits for them, and re-layouts  3.09 us
    concatenate x3, local copies, waits for them, and re-layouts, body(): jnp.concatenate([sample_taps.astype(F32), fraction, modulation[None]], ax...  2.16 us

profile of v1, /device:TPU:1, one launch (start us, length us, event | category | flops | bytes accessed | tf_op | source)
XLA Modules:
  0.0 74.7 jit_solution(8790368633137603270)
XLA Ops:
  0.6 1.0 %concatenate.12 = f32[1,27,256]{2,1,0:T(8,128)S(1)} reshape(f32[9,24,32]{2,1,0:T(8,128)} %param.11) | data formatting | bytes 55296 | tf_op jit(solution)/shard_map/concatenate | solution.py:340
  1.6 1.1 %concatenate.11 = f32[2,27,256]{2,1,0:T(8,128)S(1)} reshape(f32[2,9,24,32]{3,2,1,0:T(8,128)} %param.10) | data formatting | bytes 110592 | tf_op jit(solution)/shard_map/concatenate | solution.py:340
  2.7 1.0 %convert_element_type.3 = f32[2,9,24,32]{3,2,1,0:T(8,128)S(1)} convert(s32[2,9,24,32]{3,2,1,0:T(8,128)} %param.9) | non-fusion elementwise | flops 13824 | bytes 110592 | tf_op jit(solution)/shard_map/convert_element_type | solution.py:340
  3.6 0.1 concatenate.10
  3.8 0.7 pad_maximum_fusion.aux
  4.4 67.2 %deform_backward.1 = (bf16[24,32,256]{2,1,0:T(8,128)(2,1)}, f32[32,72]{1,0:T(8,128)}) custom-call(f32[5,27,256]{2,1,0:T(8,128)} %pad_maximum_fusion.aux, bf16[24,32,256]{2,1,0:T(8,128)(2,1)} %feat.1, bf16[768,256]{1,0:T(8,128)(2,1)} %bitcast.5, bf16[9,256,256]{2,1,0:T(8,128)(2,1)} %wgt.1), custom_call_target="tpu_custom_call" | custom-call | flops 22000001024 | bytes 8000000 | tf_op jit(solution)/shard_map/deform_backward/pallas_call | solution.py:344
  71.6 1.8 %copy.10 = bf16[24,32,256]{2,1,0:T(8,128)(2,1)} copy(bf16[24,32,256]{2,1,0:T(8,128)(2,1)} %get-tuple-element.4) | data formatting | bytes 786432
  73.4 1.3 %copy.11 = f32[32,72]{1,0:T(8,128)} copy(f32[32,72]{1,0:T(8,128)} %get-tuple-element.5) | data formatting | bytes 18432

commit v2 on v1

--- a/solution.py
+++ b/solution.py
@@ -19,7 +19,6 @@
 WR, WC = TR + 2 * RIM, 64
 STRIP = 8
 REACH = STRIP + 2 * RIM
-CHUNK = 6
 NROW, NCOL = 32, 8
 BLOCK = TAPS * CH // NROW
 HALF = CH // NCOL // 2
@@ -38,9 +37,9 @@
 
 
 def kernel(
-    aux, feat, gout, wgt,
+    taps, frac, mask, feat, gout, wgt,
     gx, gw,
-    r_ref, c_ref, e_ref, gcol, gt,
+    aux, r_ref, c_ref, e_ref, gcol, gt,
     xbuf, ext, fwin, ft, fte,
     acc, acce, gsend, grecv, xf, csend, crecv,
     gbuf, rbuf, own, sbuf, cbuf, tbuf, dbuf,
@@ -69,28 +68,6 @@
 
     lax.fori_loop(1, NROW, greet_row, 0)
     lax.fori_loop(1, NCOL, greet_col, 0)
-
-    row0 = (me_r * TR - RIM).astype(F32)
-    col0 = (me_c * TC - 16).astype(F32)
-
-    def hats(ks, carry):
-        r = aux[0, pl.ds(ks, 1), :] - row0
-        s = aux[1, pl.ds(ks, 1), :] - col0
-        fy, fx = aux[2, pl.ds(ks, 1), :], aux[3, pl.ds(ks, 1), :]
-        m = aux[4, pl.ds(ks, 1), :]
-        ids = iota((64, 256), 0).astype(F32)
-        r_ref[ks] = jnp.where(ids == r, m * (1.0 - fy), jnp.where(ids == r + 1.0, m * fy, 0.0))
-        c_ref[ks] = jnp.where(ids == s, 1.0 - fx, jnp.where(ids == s + 1.0, fx, 0.0))
-        e_ref[ks, pl.ds(0, 1)] = jnp.where(s == -1.0, 1.0 - fx, 0.0)
-        e_ref[ks, pl.ds(1, 1)] = jnp.where(s == 63.0, fx, 0.0)
-        return carry
-
-    lax.fori_loop(0, 27, hats, 0)
-
-    pick = iota((64, 768), 0)
-    pick = TC * lax.rem(pick, 32) + 15 + lax.div(pick, 32)
-    picked = (iota((64, 768), 1) == pick).astype(BF16)
-    xbuf[...] = dot(picked, feat[...].reshape(768, CH)).astype(BF16).reshape(2, 32, CH)
 
     f_copies = [
         remote(feat.at[:, pl.ds(16, 16)], fwin.at[pl.ds(RIM, TR), pl.ds(0, 16)], f_send.at[0], f_recv.at[0], (me_r, right)),
@@ -108,59 +85,82 @@
     ]
 
     pl.semaphore_wait(barrier, NROW + NCOL - 2)
-    for copy in f_copies[:6]:
+    for copy in (f_copies[0], f_copies[1], f_copies[4], f_copies[5]):
         copy.start()
+    pick = iota((64, 768), 0)
+    pick = TC * lax.rem(pick, 32) + 15 + lax.div(pick, 32)
+    picked = (iota((64, 768), 1) == pick).astype(BF16)
+    xbuf[...] = dot(picked, feat[...].reshape(768, CH)).astype(BF16).reshape(2, 32, CH)
+    f_copies[2].start()
+    f_copies[3].start()
     fwin[RIM : RIM + TR, 16 : 16 + TC] = feat[...]
 
-    def grad_cols(k, carry):
+    for n in range(5):
+        ref, at = ((taps, 0), (taps, 1), (frac, 0), (frac, 1), (mask, 0))[n]
+        pieces = [ref[at, pl.ds(row, 27, stride=STRIP), :].astype(F32) for row in range(STRIP)]
+        aux[n, 0:27] = jnp.concatenate(pieces, axis=1)
+
+    row0 = (me_r * TR - RIM).astype(F32)
+    col0 = (me_c * TC - 16).astype(F32)
+
+    def hats(ks, carry):
+        r = aux[0, pl.ds(ks, 1), :] - row0
+        s = aux[1, pl.ds(ks, 1), :] - col0
+        fy, fx = aux[2, pl.ds(ks, 1), :], aux[3, pl.ds(ks, 1), :]
+        m = aux[4, pl.ds(ks, 1), :]
+        ids = iota((64, 256), 0).astype(F32)
+        r_ref[ks] = jnp.where(ids == r, m * (1.0 - fy), jnp.where(ids == r + 1.0, m * fy, 0.0))
+        c_ref[ks] = jnp.where(ids == s, 1.0 - fx, jnp.where(ids == s + 1.0, fx, 0.0))
+        e_ref[ks, pl.ds(0, 1)] = jnp.where(s == -1.0, 1.0 - fx, 0.0)
+        e_ref[ks, pl.ds(1, 1)] = jnp.where(s == 63.0, fx, 0.0)
+        return carry
+
+    lax.fori_loop(0, 27, hats, 0)
+
+
+    for k in range(TAPS):
         gcol[k] = dot(gout[...], wgt[k], NT).astype(BF16)
-        return carry
-
-    lax.fori_loop(0, TAPS, grad_cols, 0)
-    eye = (iota((CH, CH), 0) == iota((CH, CH), 1)).astype(BF16)
-    gt[...] = dot(eye, gout[...], NT).astype(BF16)
-    acc[...] = jnp.zeros_like(acc)
-    acce[...] = jnp.zeros_like(acce)
-
-    def block(ks, i0, n):
+    gt[...] = gout[...].T
+
+    def block(ks, rows):
         c = c_ref[ks]
-        return jnp.concatenate([(r_ref[ks, pl.ds(i0 + a, 1), :] * c).astype(BF16) for a in range(n)], axis=0)
+        return jnp.concatenate([(r_ref[ks, i : i + 1, :] * c).astype(BF16) for i in rows], axis=0)
 
     def edge(ks):
         r = r_ref[ks]
-        return jnp.concatenate([(r * e_ref[ks, pl.ds(e, 1), :]).astype(BF16) for e in range(2)], axis=0)
-
-    def scatter(s):
-        rows = pl.ds(pl.multiple_of(256 * s, 256), 256)
-
-        def step(q, carry):
-            i0 = STRIP * s + q * CHUNK
-            cells = pl.ds(pl.multiple_of(i0 * WC, WC), CHUNK * WC)
-            total = acc[cells, :]
-            for k in range(TAPS):
-                total = total + dot(block(3 * k + s, i0, CHUNK), gcol[k, rows, :])
-            acc[cells, :] = total
-            return carry
-
-        lax.fori_loop(0, REACH // CHUNK, step, 0)
-        total = acce[...]
+        return jnp.concatenate([(r * e_ref[ks, e : e + 1, :]).astype(BF16) for e in range(2)], axis=0)
+
+    def scatter(total, s, rows):
         for k in range(TAPS):
-            total = total + dot(edge(3 * k + s), gcol[k, rows, :])
-        acce[...] = total
-
-    scatter(0)
+            part = dot(block(3 * k + s, rows), gcol[k, 256 * s : 256 * s + 256, :])
+            total = part if total is None else total + part
+        return total
+
+    def add_cells(first, value):
+        cells = slice(first * WC, first * WC + value.shape[0])
+        acc[cells, :] = acc[cells, :] + value
+
+    rim = RIM * WC
+    acc[:rim] = jnp.zeros((rim, CH), F32)
+    acc[(RIM + TR) * WC :] = jnp.zeros((rim, CH), F32)
+    for s in range(3):
+        above = range(STRIP * s, RIM)
+        below = range(RIM + TR, STRIP * s + REACH)
+        total = scatter(None, s, [*above, *below])
+        add_cells(above[0], total[: len(above) * WC])
+        add_cells(below[0], total[len(above) * WC :])
+    total = None
+    for s in range(3):
+        for k in range(TAPS):
+            part = dot(edge(3 * k + s), gcol[k, 256 * s : 256 * s + 256, :])
+            total = part if total is None else total + part
+    acce[...] = total
+
     for copy in f_copies[:4]:
         copy.wait_recv()
     for copy in f_copies[6:]:
         copy.start()
 
-    def rest(s, carry):
-        scatter(s)
-        return carry
-
-    lax.fori_loop(1, 3, rest, 0)
-
-    rim = RIM * WC
     gsend[0, :rim] = acc[:rim].astype(BF16)
     gsend[1, :rim] = acc[(RIM + TR) * WC :].astype(BF16)
     for e in range(2):
@@ -175,21 +175,21 @@
     g_copies[0].start()
     g_copies[1].start()
 
+    total = None
+    for s in range(3):
+        total = scatter(total, s, range(RIM, RIM + TR))
+    acc[rim : rim + TR * WC] = total
+
     for copy in f_copies[4:]:
         copy.wait_recv()
-
-    def turn(q, carry):
-        rows = fwin[pl.ds(2 * q, 2)].reshape(2 * WC, CH)
-        ft[:, pl.ds(pl.multiple_of(q * 2 * WC, 2 * WC), 2 * WC)] = dot(eye, rows, NT).astype(BF16)
-        return carry
-
-    lax.fori_loop(0, WR // 2, turn, 0)
+    for q in range(WR // 2):
+        ft[:, 2 * WC * q : 2 * WC * q + 2 * WC] = fwin[2 * q : 2 * q + 2].reshape(2 * WC, CH).T
     at = iota((128, 192), 0)
     side, i = lax.div(at, 64), lax.rem(at, 64)
     slot = jnp.where(i < RIM, 64 + 7 + i, jnp.where(i < RIM + TR, i - RIM, 128 + i - RIM - TR)) + 32 * side
     chosen = ((iota((128, 192), 1) == slot) & (i < WR)).astype(BF16)
     edges = dot(chosen, ext[...].reshape(192, CH)).astype(BF16)
-    fte[...] = dot(eye, edges, NT).astype(BF16)
+    fte[...] = edges.T
 
     def sibling_copy(k):
         return remote(gbuf.at[k, 1 - core], rbuf.at[k], s1_send.at[k], s1_recv.at[k], (sibling, me_c))
@@ -239,10 +239,10 @@
             for q in range(11):
                 at = STRIP * WC * s + 256 * q
                 if q < 10:
-                    lhs, rhs = ft[:, at : at + 256], block(ks, STRIP * s + 4 * q, 4)
+                    lhs, rhs = ft[:, at : at + 256], block(ks, range(STRIP * s + 4 * q, STRIP * s + 4 * q + 4))
                 else:
                     lhs = jnp.concatenate([ft[:, at : at + 128], fte[...]], axis=1)
-                    rhs = jnp.concatenate([block(ks, STRIP * s + 40, 2), edge(ks)], axis=0)
+                    rhs = jnp.concatenate([block(ks, range(STRIP * s + 40, STRIP * s + 42)), edge(ks)], axis=0)
                 part = dot(lhs, rhs)
                 total = part if total is None else total + part
             part = dot(gt[:, 256 * s : 256 * s + 256], total.astype(BF16), NT)
@@ -337,8 +337,6 @@
 
 
 def body(features, grad_out, weight, sample_taps, fraction, modulation):
-    aux = jnp.concatenate([sample_taps.astype(F32), fraction, modulation[None]], axis=0)
-    aux = aux.reshape(5, 27, 256)
     vmem = pl.BlockSpec(memory_space=pltpu.VMEM)
     dma = pltpu.SemaphoreType.DMA
     return pl.pallas_call(
@@ -348,9 +346,10 @@
             jax.ShapeDtypeStruct((TR, TC, CH), BF16),
             jax.ShapeDtypeStruct((2 * HALF, BLOCK), F32),
         ),
-        in_specs=[vmem] * 4,
+        in_specs=[vmem] * 6,
         out_specs=(vmem, vmem),
         scratch_shapes=[
+            pltpu.VMEM((5, 32, 256), F32),
             pltpu.VMEM((27, 64, 256), F32),
             pltpu.VMEM((27, 64, 256), F32),
             pltpu.VMEM((27, 8, 256), F32),
@@ -383,7 +382,14 @@
             collective_id=0, has_side_effects=True, vmem_limit_bytes=56 * 2**20
         ),
         cost_estimate=pl.CostEstimate(flops=22 * 10**9, bytes_accessed=8 * 10**6, transcendentals=0),
-    )(aux, features, grad_out.reshape(768, CH), weight)
+    )(
+        sample_taps.reshape(2, 9 * TR, TC),
+        fraction.reshape(2, 9 * TR, TC),
+        modulation.reshape(1, 9 * TR, TC),
+        features,
+        grad_out.reshape(768, CH),
+        weight,
+    )
 
 
 def solution(mesh):

time: 75 us -> 67.9 us (0.905)
  Pallas kernels: 67.2 us -> 63.9 us
  local copies, waits for them, and re-layouts: 5.25 us -> 3.09 us
  other arithmetic: 1.63 us -> 0 us
    pallas_call x1, Pallas kernels: 67.2 us -> 63.9 us  [body(): pl.pallas_call(kernel, name='deform_backward', out_shape=(jax.ShapeDtypeS...]
    concatenate x3 -> x0, local copies, waits for them, and re-layouts: 2.16 us -> none  [body(): jnp.concatenate([sample_taps.astype(F32), fraction, modulation[None]], ax...]
    convert_element_type x1 -> x0, other arithmetic: 0.95 us -> none  [body(): sample_taps.astype(F32)]
where the time goes in v2:
time: 67.9 us; the launch traced here: 67.7 us
  Pallas kernels  63.9 us (94%)
  local copies, waits for them, and re-layouts  3.09 us (5%)
    pallas_call x1, Pallas kernels, body(): pl.pallas_call(kernel, name='deform_backward', out_shape=(jax.ShapeDtypeS...  63.9 us
    unnamed x2, local copies, waits for them, and re-layouts  3.09 us

profile of v2, /device:TPU:1, one launch (start us, length us, event | category | flops | bytes accessed | tf_op | source)
XLA Modules:
  0.0 67.7 jit_solution(2555701694688080745)
XLA Ops:
  0.6 63.9 %deform_backward.1 = (bf16[24,32,256]{2,1,0:T(8,128)(2,1)}, f32[32,72]{1,0:T(8,128)}) custom-call(s32[2,216,32]{2,1,0:T(8,128)} %bitcast.5, f32[2,216,32]{2,1,0:T(8,128)} %bitcast.6, f32[1,216,32]{2,1,0:T(8,128)} %bitcast.7, bf16[24,32,256]{2,1,0:T(8,128)(2,1)} %feat.1, bf16[768,256]{1,0:T(8,128)(2,1)} %bitcast.4, bf16[9,256,256]{2,1,0:T(8,128)(2,1)} %wgt.1), custom_call_target="tpu_custom_call" | custom-call | flops 22000001024 | bytes 8000000 | tf_op jit(solution)/shard_map/deform_backward/pallas_call | solution.py:342
  64.6 1.8 %copy.10 = bf16[24,32,256]{2,1,0:T(8,128)(2,1)} copy(bf16[24,32,256]{2,1,0:T(8,128)(2,1)} %get-tuple-element.4) | data formatting | bytes 786432
  66.4 1.3 %copy.11 = f32[32,72]{1,0:T(8,128)} copy(f32[32,72]{1,0:T(8,128)} %get-tuple-element.5) | data formatting | bytes 18432

commit v3 on v2

--- a/solution.py
+++ b/solution.py
@@ -20,8 +20,16 @@
 STRIP = 8
 REACH = STRIP + 2 * RIM
 NROW, NCOL = 32, 8
+EARLY = 6
 BLOCK = TAPS * CH // NROW
 HALF = CH // NCOL // 2
+
+
+OWN_ROWS = list(range(RIM, RIM + TR))
+
+
+def rim_rows(s):
+    return [*range(STRIP * s, RIM), *range(RIM + TR, STRIP * s + REACH)]
 
 
 def dot(a, b, dims=NN):
@@ -40,7 +48,7 @@
     taps, frac, mask, feat, gout, wgt,
     gx, gw,
     aux, r_ref, c_ref, e_ref, gcol, gt,
-    xbuf, ext, fwin, ft, fte,
+    xbuf, ext, fwin, ft, fth, partial,
     acc, acce, gsend, grecv, xf, csend, crecv,
     gbuf, rbuf, own, sbuf, cbuf, tbuf, dbuf,
     f_send, f_recv, g_send, g_recv, s1_send, s1_recv, s2_send, s2_recv, s3_send, s3_recv,
@@ -66,8 +74,11 @@
         pl.semaphore_signal(barrier, inc=1, device_id=(me_r, mod(me_c + d, NCOL)), device_id_type=MESH)
         return carry
 
-    lax.fori_loop(1, NROW, greet_row, 0)
-    lax.fori_loop(1, NCOL, greet_col, 0)
+    for d in (1, -1):
+        greet_row(d, 0)
+        greet_col(d, 0)
+    lax.fori_loop(2, NCOL - 1, greet_col, 0)
+    lax.fori_loop(2, NROW - 1, greet_row, 0)
 
     f_copies = [
         remote(feat.at[:, pl.ds(16, 16)], fwin.at[pl.ds(RIM, TR), pl.ds(0, 16)], f_send.at[0], f_recv.at[0], (me_r, right)),
@@ -144,22 +155,16 @@
     acc[:rim] = jnp.zeros((rim, CH), F32)
     acc[(RIM + TR) * WC :] = jnp.zeros((rim, CH), F32)
     for s in range(3):
-        above = range(STRIP * s, RIM)
-        below = range(RIM + TR, STRIP * s + REACH)
-        total = scatter(None, s, [*above, *below])
-        add_cells(above[0], total[: len(above) * WC])
-        add_cells(below[0], total[len(above) * WC :])
+        above = (RIM - STRIP * s) * WC
+        total = scatter(None, s, rim_rows(s))
+        add_cells(STRIP * s, total[:above])
+        add_cells(RIM + TR, total[above:])
     total = None
     for s in range(3):
         for k in range(TAPS):
             part = dot(edge(3 * k + s), gcol[k, 256 * s : 256 * s + 256, :])
             total = part if total is None else total + part
     acce[...] = total
-
-    for copy in f_copies[:4]:
-        copy.wait_recv()
-    for copy in f_copies[6:]:
-        copy.start()
 
     gsend[0, :rim] = acc[:rim].astype(BF16)
     gsend[1, :rim] = acc[(RIM + TR) * WC :].astype(BF16)
@@ -172,24 +177,45 @@
         remote(csend.at[0], crecv.at[0], g_send.at[2], g_recv.at[2], (me_r, left)),
         remote(csend.at[1], crecv.at[1], g_send.at[3], g_recv.at[3], (me_r, right)),
     ]
+    acc[rim : rim + TR * WC] = scatter(None, 0, OWN_ROWS)
+
+    for copy in f_copies[:4]:
+        copy.wait_recv()
+    for copy in f_copies[6:]:
+        copy.start()
     g_copies[0].start()
     g_copies[1].start()
 
-    total = None
-    for s in range(3):
-        total = scatter(total, s, range(RIM, RIM + TR))
-    acc[rim : rim + TR * WC] = total
+    def turned(rows):
+        pair = jnp.concatenate([fwin[rows[0]], fwin[rows[1]]], axis=0)
+        return pair.T
+
+    for q in range(TR // 2):
+        ft[:, 2 * WC * q : 2 * WC * q + 2 * WC] = turned(OWN_ROWS[2 * q : 2 * q + 2])
+
+    def gather_own(k, carry):
+        for s in range(3):
+            total = None
+            for q in range(TR // 4):
+                piece = dot(ft[:, 256 * q : 256 * q + 256], block(3 * k + s, OWN_ROWS[4 * q : 4 * q + 4]))
+                total = piece if total is None else total + piece
+            partial[3 * k + s] = total
+        return carry
+
+    lax.fori_loop(0, TAPS, gather_own, 0)
 
     for copy in f_copies[4:]:
         copy.wait_recv()
-    for q in range(WR // 2):
-        ft[:, 2 * WC * q : 2 * WC * q + 2 * WC] = fwin[2 * q : 2 * q + 2].reshape(2 * WC, CH).T
     at = iota((128, 192), 0)
     side, i = lax.div(at, 64), lax.rem(at, 64)
     slot = jnp.where(i < RIM, 64 + 7 + i, jnp.where(i < RIM + TR, i - RIM, 128 + i - RIM - TR)) + 32 * side
     chosen = ((iota((128, 192), 1) == slot) & (i < WR)).astype(BF16)
-    edges = dot(chosen, ext[...].reshape(192, CH)).astype(BF16)
-    fte[...] = edges.T
+    edges = dot(chosen, ext[...].reshape(192, CH)).astype(BF16).T
+    for s in range(3):
+        rows = rim_rows(s)
+        for q in range(len(rows) // 2):
+            fth[s, :, 2 * WC * q : 2 * WC * q + 2 * WC] = turned(rows[2 * q : 2 * q + 2])
+        fth[s, :, len(rows) * WC :] = edges
 
     def sibling_copy(k):
         return remote(gbuf.at[k, 1 - core], rbuf.at[k], s1_send.at[k], s1_recv.at[k], (sibling, me_c))
@@ -234,19 +260,15 @@
     def tap(k, carry):
         total_w = None
         for s in range(3):
-            ks = 3 * k + s
-            total = None
-            for q in range(11):
-                at = STRIP * WC * s + 256 * q
-                if q < 10:
-                    lhs, rhs = ft[:, at : at + 256], block(ks, range(STRIP * s + 4 * q, STRIP * s + 4 * q + 4))
-                else:
-                    lhs = jnp.concatenate([ft[:, at : at + 128], fte[...]], axis=1)
-                    rhs = jnp.concatenate([block(ks, range(STRIP * s + 40, STRIP * s + 42)), edge(ks)], axis=0)
-                part = dot(lhs, rhs)
-                total = part if total is None else total + part
-            part = dot(gt[:, 256 * s : 256 * s + 256], total.astype(BF16), NT)
-            total_w = part if total_w is None else total_w + part
+            ks, rows = 3 * k + s, rim_rows(s)
+            total = partial[ks]
+            for q in range(5):
+                rhs = block(ks, rows[4 * q : 4 * q + 4])
+                if q == 4:
+                    rhs = jnp.concatenate([rhs, edge(ks)], axis=0)
+                total = total + dot(fth[s, :, 256 * q : 256 * q + 256], rhs)
+            piece = dot(gt[:, 256 * s : 256 * s + 256], total.astype(BF16), NT)
+            total_w = piece if total_w is None else total_w + piece
         cut = total_w.reshape(NCOL, 2, HALF, CH)
         gbuf[k, 0] = cut[:, 0]
         gbuf[k, 1] = cut[:, 1]
@@ -256,14 +278,47 @@
         def _():
             pass_on(k - 1)
 
-        @pl.when(k == 4)
+        return carry
+
+    lax.fori_loop(0, TAPS, tap, 0)
+    add_cells(RIM, scatter(None, 1, OWN_ROWS))
+    pass_on(TAPS - 1)
+    add_cells(RIM, scatter(None, 2, OWN_ROWS))
+    fold_rows()
+
+    def gather_cols(k, carry):
+        total = rbuf[k, me_c]
+        for d in range(1, NCOL):
+            col_copy(k, d).wait_recv()
+            total = total + cbuf[k, d - 1].astype(F32)
+        own[k] = total
+        return carry
+
+    def row_copy(d):
+        to = mod(me_r + d, NROW)
+        return remote(tbuf.at[to], dbuf.at[d - 1], s3_send.at[d - 1], s3_recv.at[d - 1], (to, me_c))
+
+    def send_row(b, carry):
+        d = mod(b - me_r, NROW)
+
+        @pl.when(d > 0)
         def _():
-            fold_rows()
-
-        return carry
-
-    lax.fori_loop(0, TAPS, tap, 0)
-    pass_on(TAPS - 1)
+            row_copy(d).start()
+
+        return carry
+
+    def send_blocks(first, last, flat, base):
+        for b in range(first, last):
+            tbuf[b] = flat[:, BLOCK * b - base : BLOCK * b - base + 128].astype(BF16)
+        lax.fori_loop(first, last, send_row, 0)
+
+    early = EARLY * CH // BLOCK
+    lax.fori_loop(0, EARLY, gather_cols, 0)
+    flat = [own[k] for k in range(EARLY)] + [jnp.zeros((HALF, 128), F32)]
+    send_blocks(0, early, jnp.concatenate(flat, axis=1), 0)
+    lax.fori_loop(EARLY, TAPS, gather_cols, 0)
+    flat = [own[k] for k in range(EARLY - 1, TAPS)] + [jnp.zeros((HALF, 128), F32)]
+    send_blocks(early, NROW, jnp.concatenate(flat, axis=1), (EARLY - 1) * CH)
 
     g_copies[2].wait_recv()
     g_copies[3].wait_recv()
@@ -280,29 +335,6 @@
         return carry
 
     lax.fori_loop(0, TR, finish, 0)
-
-    def gather_cols(k, carry):
-        total = rbuf[k, me_c]
-        for d in range(1, NCOL):
-            col_copy(k, d).wait_recv()
-            total = total + cbuf[k, d - 1].astype(F32)
-        own[k] = total
-        return carry
-
-    lax.fori_loop(0, TAPS, gather_cols, 0)
-    flat = jnp.concatenate([own[k] for k in range(TAPS)] + [jnp.zeros((HALF, 128), F32)], axis=1)
-    for b in range(NROW):
-        tbuf[b] = flat[:, BLOCK * b : BLOCK * b + 128].astype(BF16)
-
-    def row_copy(d):
-        to = mod(me_r + d, NROW)
-        return remote(tbuf.at[to], dbuf.at[d - 1], s3_send.at[d - 1], s3_recv.at[d - 1], (to, me_c))
-
-    def send_row(d, carry):
-        row_copy(d).start()
-        return carry
-
-    lax.fori_loop(1, NROW, send_row, 0)
 
     def gather_rows(d, carry):
         row_copy(d).wait_recv()
@@ -358,8 +390,9 @@
             pltpu.VMEM((2, 32, CH), BF16),
             pltpu.VMEM((3, 2, 32, CH), BF16),
             pltpu.VMEM((WR, WC, CH), BF16),
-            pltpu.VMEM((CH, WR * WC), BF16),
-            pltpu.VMEM((CH, 128), BF16),
+            pltpu.VMEM((CH, TR * WC), BF16),
+            pltpu.VMEM((3, CH, 18 * WC + 128), BF16),
+            pltpu.VMEM((27, CH, 256), F32),
             pltpu.VMEM((WR * WC, CH), F32),
             pltpu.VMEM((128, CH), F32),
             pltpu.VMEM((2, RIM * WC + 64, CH), BF16),

time: 67.9 us -> 65.4 us (0.963)
  Pallas kernels: 63.9 us -> 61.4 us
    pallas_call x1, Pallas kernels: 63.9 us -> 61.4 us  [body(): pl.pallas_call(kernel, name='deform_backward', out_shape=(jax.ShapeDtypeS...]
where the time goes in v3:
time: 65.4 us; the launch traced here: 65.2 us
  Pallas kernels  61.4 us (94%)
  local copies, waits for them, and re-layouts  3.09 us (5%)
    pallas_call x1, Pallas kernels, body(): pl.pallas_call(kernel, name='deform_backward', out_shape=(jax.ShapeDtypeS...  61.4 us
    unnamed x2, local copies, waits for them, and re-layouts  3.09 us

profile of v3, /device:TPU:1, one launch (start us, length us, event | category | flops | bytes accessed | tf_op | source)
XLA Modules:
  0.0 65.2 jit_solution(11187081647623338799)
XLA Ops:
  0.6 61.4 %deform_backward.1 = (bf16[24,32,256]{2,1,0:T(8,128)(2,1)}, f32[32,72]{1,0:T(8,128)}) custom-call(s32[2,216,32]{2,1,0:T(8,128)} %bitcast.5, f32[2,216,32]{2,1,0:T(8,128)} %bitcast.6, f32[1,216,32]{2,1,0:T(8,128)} %bitcast.7, bf16[24,32,256]{2,1,0:T(8,128)(2,1)} %feat.1, bf16[768,256]{1,0:T(8,128)(2,1)} %bitcast.4, bf16[9,256,256]{2,1,0:T(8,128)(2,1)} %wgt.1), custom_call_target="tpu_custom_call" | custom-call | flops 22000001024 | bytes 8000000 | tf_op jit(solution)/shard_map/deform_backward/pallas_call | solution.py:374
  62.1 1.8 %copy.10 = bf16[24,32,256]{2,1,0:T(8,128)(2,1)} copy(bf16[24,32,256]{2,1,0:T(8,128)(2,1)} %get-tuple-element.4) | data formatting | bytes 786432
  63.8 1.3 %copy.11 = f32[32,72]{1,0:T(8,128)} copy(f32[32,72]{1,0:T(8,128)} %get-tuple-element.5) | data formatting | bytes 18432

commit v4 on v3

--- a/solution.py
+++ b/solution.py
@@ -45,10 +45,10 @@
 
 
 def kernel(
-    taps, frac, mask, feat, gout, wgt,
+    taps_in, frac_in, mask_in, feat, gout_in, wgt_in,
     gx, gw,
-    aux, r_ref, c_ref, e_ref, gcol, gt,
-    xbuf, ext, fwin, ft, fth, partial,
+    taps, frac, mask, gout, wgt, in_sem, aux, r_ref, c_ref, e_ref, gcol, gt,
+    xbuf, ext, fwin, ft, fth, partial, col,
     acc, acce, gsend, grecv, xf, csend, crecv,
     gbuf, rbuf, own, sbuf, cbuf, tbuf, dbuf,
     f_send, f_recv, g_send, g_recv, s1_send, s1_recv, s2_send, s2_recv, s3_send, s3_recv,
@@ -79,6 +79,16 @@
         greet_col(d, 0)
     lax.fori_loop(2, NCOL - 1, greet_col, 0)
     lax.fori_loop(2, NROW - 1, greet_row, 0)
+
+    home = fwin.at[pl.ds(RIM, TR), pl.ds(16, TC)]
+    loads = [
+        pltpu.make_async_copy(src, dst, in_sem.at[n])
+        for n, (src, dst) in enumerate(
+            ((feat, home), (taps_in, taps), (frac_in, frac), (mask_in, mask), (gout_in, gout), (wgt_in, wgt))
+        )
+    ]
+    for load in loads:
+        load.start()
 
     f_copies = [
         remote(feat.at[:, pl.ds(16, 16)], fwin.at[pl.ds(RIM, TR), pl.ds(0, 16)], f_send.at[0], f_recv.at[0], (me_r, right)),
@@ -101,10 +111,12 @@
     pick = iota((64, 768), 0)
     pick = TC * lax.rem(pick, 32) + 15 + lax.div(pick, 32)
     picked = (iota((64, 768), 1) == pick).astype(BF16)
-    xbuf[...] = dot(picked, feat[...].reshape(768, CH)).astype(BF16).reshape(2, 32, CH)
+    loads[0].wait()
+    xbuf[...] = dot(picked, home[...].reshape(768, CH)).astype(BF16).reshape(2, 32, CH)
     f_copies[2].start()
     f_copies[3].start()
-    fwin[RIM : RIM + TR, 16 : 16 + TC] = feat[...]
+    for load in loads[1:4]:
+        load.wait()
 
     for n in range(5):
         ref, at = ((taps, 0), (taps, 1), (frac, 0), (frac, 1), (mask, 0))[n]
@@ -114,57 +126,61 @@
     row0 = (me_r * TR - RIM).astype(F32)
     col0 = (me_c * TC - 16).astype(F32)
 
-    def hats(ks, carry):
-        r = aux[0, pl.ds(ks, 1), :] - row0
-        s = aux[1, pl.ds(ks, 1), :] - col0
-        fy, fx = aux[2, pl.ds(ks, 1), :], aux[3, pl.ds(ks, 1), :]
-        m = aux[4, pl.ds(ks, 1), :]
-        ids = iota((64, 256), 0).astype(F32)
-        r_ref[ks] = jnp.where(ids == r, m * (1.0 - fy), jnp.where(ids == r + 1.0, m * fy, 0.0))
-        c_ref[ks] = jnp.where(ids == s, 1.0 - fx, jnp.where(ids == s + 1.0, fx, 0.0))
-        e_ref[ks, pl.ds(0, 1)] = jnp.where(s == -1.0, 1.0 - fx, 0.0)
-        e_ref[ks, pl.ds(1, 1)] = jnp.where(s == 63.0, fx, 0.0)
-        return carry
-
-    lax.fori_loop(0, 27, hats, 0)
-
-
+    ids = iota((64, 256), 0).astype(F32)
+    def hats(k, carry):
+        for ks in (3 * k, 3 * k + 1, 3 * k + 2):
+            at = pl.ds(ks, 1)
+            r, c = aux[0, at, :] - row0, aux[1, at, :] - col0
+            fy, fx, m = (aux[n, at, :] for n in (2, 3, 4))
+            r_ref[ks] = jnp.where(ids == r, m * (1.0 - fy), jnp.where(ids == r + 1.0, m * fy, 0.0))
+            c_ref[ks] = jnp.where(ids == c, 1.0 - fx, jnp.where(ids == c + 1.0, fx, 0.0))
+            e_ref[ks, 0:1] = jnp.where(c == -1.0, 1.0 - fx, 0.0)
+            e_ref[ks, 1:2] = jnp.where(c == 63.0, fx, 0.0)
+        return carry
+
+    lax.fori_loop(0, TAPS, hats, 0)
+
+    loads[4].wait()
+    loads[5].wait()
     for k in range(TAPS):
         gcol[k] = dot(gout[...], wgt[k], NT).astype(BF16)
     gt[...] = gout[...].T
 
     def block(ks, rows):
         c = c_ref[ks]
-        return jnp.concatenate([(r_ref[ks, i : i + 1, :] * c).astype(BF16) for i in rows], axis=0)
+        return jnp.concatenate([(r_ref[ks, pl.ds(i, 1), :] * c).astype(BF16) for i in rows], axis=0)
 
     def edge(ks):
         r = r_ref[ks]
         return jnp.concatenate([(r * e_ref[ks, e : e + 1, :]).astype(BF16) for e in range(2)], axis=0)
 
+    def strip_of(s):
+        return pl.ds(pl.multiple_of(256 * s, 256), 256)
+
     def scatter(total, s, rows):
         for k in range(TAPS):
-            part = dot(block(3 * k + s, rows), gcol[k, 256 * s : 256 * s + 256, :])
+            part = dot(block(3 * k + s, rows), gcol[k, strip_of(s), :])
             total = part if total is None else total + part
         return total
 
-    def add_cells(first, value):
-        cells = slice(first * WC, first * WC + value.shape[0])
-        acc[cells, :] = acc[cells, :] + value
-
     rim = RIM * WC
-    acc[:rim] = jnp.zeros((rim, CH), F32)
-    acc[(RIM + TR) * WC :] = jnp.zeros((rim, CH), F32)
-    for s in range(3):
-        above = (RIM - STRIP * s) * WC
-        total = scatter(None, s, rim_rows(s))
-        add_cells(STRIP * s, total[:above])
-        add_cells(RIM + TR, total[above:])
-    total = None
-    for s in range(3):
+    acc[...] = jnp.zeros_like(acc)
+    acce[...] = jnp.zeros_like(acce)
+
+    def scatter_rim(s, carry):
+        rows = [STRIP * s + t for t in range(18)]
+        rows = [row + jnp.where(row < RIM, 0, TR) for row in rows]
+        total = scatter(None, s, rows)
+        for t, row in enumerate(rows):
+            cells = pl.ds(pl.multiple_of(row * WC, WC), WC)
+            acc[cells, :] = acc[cells, :] + total[WC * t : WC * t + WC]
+        total = acce[...]
         for k in range(TAPS):
-            part = dot(edge(3 * k + s), gcol[k, 256 * s : 256 * s + 256, :])
-            total = part if total is None else total + part
-    acce[...] = total
+            total = total + dot(edge(3 * k + s), gcol[k, strip_of(s), :])
+        acce[...] = total
+        return carry
+
+    lax.fori_loop(0, 3, scatter_rim, 0)
 
     gsend[0, :rim] = acc[:rim].astype(BF16)
     gsend[1, :rim] = acc[(RIM + TR) * WC :].astype(BF16)
@@ -177,7 +193,6 @@
         remote(csend.at[0], crecv.at[0], g_send.at[2], g_recv.at[2], (me_r, left)),
         remote(csend.at[1], crecv.at[1], g_send.at[3], g_recv.at[3], (me_r, right)),
     ]
-    acc[rim : rim + TR * WC] = scatter(None, 0, OWN_ROWS)
 
     for copy in f_copies[:4]:
         copy.wait_recv()
@@ -193,16 +208,16 @@
     for q in range(TR // 2):
         ft[:, 2 * WC * q : 2 * WC * q + 2 * WC] = turned(OWN_ROWS[2 * q : 2 * q + 2])
 
-    def gather_own(k, carry):
-        for s in range(3):
+    def gather_own(t, carry):
+        for ks in [9 * t + j for j in range(9)]:
             total = None
             for q in range(TR // 4):
-                piece = dot(ft[:, 256 * q : 256 * q + 256], block(3 * k + s, OWN_ROWS[4 * q : 4 * q + 4]))
+                piece = dot(ft[:, 256 * q : 256 * q + 256], block(ks, OWN_ROWS[4 * q : 4 * q + 4]))
                 total = piece if total is None else total + piece
-            partial[3 * k + s] = total
-        return carry
-
-    lax.fori_loop(0, TAPS, gather_own, 0)
+            partial[ks] = total
+        return carry
+
+    lax.fori_loop(0, 3, gather_own, 0)
 
     for copy in f_copies[4:]:
         copy.wait_recv()
@@ -257,8 +272,7 @@
         g_copies[2].start()
         g_copies[3].start()
 
-    def tap(k, carry):
-        total_w = None
+    def columns(k):
         for s in range(3):
             ks, rows = 3 * k + s, rim_rows(s)
             total = partial[ks]
@@ -267,23 +281,44 @@
                 if q == 4:
                     rhs = jnp.concatenate([rhs, edge(ks)], axis=0)
                 total = total + dot(fth[s, :, 256 * q : 256 * q + 256], rhs)
-            piece = dot(gt[:, 256 * s : 256 * s + 256], total.astype(BF16), NT)
-            total_w = piece if total_w is None else total_w + piece
-        cut = total_w.reshape(NCOL, 2, HALF, CH)
+            col[k, :, 256 * s : 256 * s + 256] = total.astype(BF16)
+
+    def kernel_grad(k):
+        cut = dot(gt[...], col[k], NT).reshape(NCOL, 2, HALF, CH)
         gbuf[k, 0] = cut[:, 0]
         gbuf[k, 1] = cut[:, 1]
-        sibling_copy(k).start()
-
-        @pl.when(k > 0)
+
+    def three_taps(t, carry):
+        a, b, c = 3 * t, 3 * t + 1, 3 * t + 2
+        columns(a)
+        columns(b)
+        kernel_grad(a)
+        columns(c)
+        kernel_grad(b)
+        kernel_grad(c)
+        for k in (a, b, c):
+            sibling_copy(k).start()
+
+        @pl.when(t > 0)
         def _():
-            pass_on(k - 1)
-
-        return carry
-
-    lax.fori_loop(0, TAPS, tap, 0)
-    add_cells(RIM, scatter(None, 1, OWN_ROWS))
-    pass_on(TAPS - 1)
-    add_cells(RIM, scatter(None, 2, OWN_ROWS))
+            for k in (a, b, c):
+                pass_on(k - 3)
+
+        return carry
+
+    lax.fori_loop(0, 3, three_taps, 0)
+
+    def scatter_own(s, carry):
+        acc[rim : rim + TR * WC] = acc[rim : rim + TR * WC] + scatter(None, s, OWN_ROWS)
+
+        @pl.when(s == 0)
+        def _():
+            for k in range(6, 9):
+                pass_on(k)
+
+        return carry
+
+    lax.fori_loop(0, 3, scatter_own, 0)
     fold_rows()
 
     def gather_cols(k, carry):
@@ -368,19 +403,30 @@
     lax.fori_loop(1, NROW, drain_row, 0)
 
 
+def hand_out(gx_in, gw_in, gx, gw):
+    gx[...] = gx_in[...]
+    gw[...] = gw_in[...]
+
+
 def body(features, grad_out, weight, sample_taps, fraction, modulation):
     vmem = pl.BlockSpec(memory_space=pltpu.VMEM)
     dma = pltpu.SemaphoreType.DMA
-    return pl.pallas_call(
+    grads = pl.pallas_call(
         kernel,
         name="deform_backward",
         out_shape=(
             jax.ShapeDtypeStruct((TR, TC, CH), BF16),
             jax.ShapeDtypeStruct((2 * HALF, BLOCK), F32),
         ),
-        in_specs=[vmem] * 6,
+        in_specs=[pl.BlockSpec(memory_space=pl.ANY)] * 6,
         out_specs=(vmem, vmem),
         scratch_shapes=[
+            pltpu.VMEM((2, 9 * TR, TC), jnp.int32),
+            pltpu.VMEM((2, 9 * TR, TC), F32),
+            pltpu.VMEM((1, 9 * TR, TC), F32),
+            pltpu.VMEM((TR * TC, CH), BF16),
+            pltpu.VMEM((TAPS, CH, CH), BF16),
+            dma((6,)),
             pltpu.VMEM((5, 32, 256), F32),
             pltpu.VMEM((27, 64, 256), F32),
             pltpu.VMEM((27, 64, 256), F32),
@@ -393,6 +439,7 @@
             pltpu.VMEM((CH, TR * WC), BF16),
             pltpu.VMEM((3, CH, 18 * WC + 128), BF16),
             pltpu.VMEM((27, CH, 256), F32),
+            pltpu.VMEM((TAPS, CH, 768), BF16),
             pltpu.VMEM((WR * WC, CH), F32),
             pltpu.VMEM((128, CH), F32),
             pltpu.VMEM((2, RIM * WC + 64, CH), BF16),
@@ -423,6 +470,13 @@
         grad_out.reshape(768, CH),
         weight,
     )
+    return pl.pallas_call(
+        hand_out,
+        name="hand_out",
+        out_shape=tuple(jax.ShapeDtypeStruct(grad.shape, grad.dtype) for grad in grads),
+        in_specs=[vmem] * 2,
+        out_specs=(vmem, vmem),
+    )(*grads)
 
 
 def solution(mesh):

time: 65.4 us -> 56.2 us (0.86)
  Pallas kernels: 61.4 us -> 55.1 us
  local copies, waits for them, and re-layouts: 3.09 us -> 0 us
    pallas_call x1, Pallas kernels: 61.4 us -> 53.3 us  [body(): pl.pallas_call(kernel, name='deform_backward', out_shape=(jax.ShapeDtypeS...]
    unnamed x2 -> x0, local copies, waits for them, and re-layouts: 3.09 us -> none
    pallas_call x0 -> x1, Pallas kernels: none -> 1.77 us  [body(): pl.pallas_call(hand_out, name='hand_out', out_shape=tuple((jax.ShapeDtype...]
where the time goes in v4:
time: 56.2 us; the launch traced here: 55.7 us
  Pallas kernels  55.1 us (98%)
  between operations  0.64 us (1%)
    pallas_call x1, Pallas kernels, body(): pl.pallas_call(kernel, name='deform_backward', out_shape=(jax.ShapeDtypeS...  53.3 us
    pallas_call x1, Pallas kernels, body(): pl.pallas_call(hand_out, name='hand_out', out_shape=tuple((jax.ShapeDtype...  1.77 us

profile of v4, /device:TPU:1, one launch (start us, length us, event | category | flops | bytes accessed | tf_op | source)
XLA Modules:
  0.0 55.7 jit_solution(15644534923053890938)
XLA Ops:
  0.6 53.3 %deform_backward.1 = (bf16[24,32,256]{2,1,0:T(8,128)(2,1)}, f32[32,72]{1,0:T(8,128)}) custom-call(s32[2,216,32]{2,1,0:T(8,128)} %bitcast.5, f32[2,216,32]{2,1,0:T(8,128)} %bitcast.6, f32[1,216,32]{2,1,0:T(8,128)} %bitcast.7, bf16[24,32,256]{2,1,0:T(8,128)(2,1)} %feat.1, bf16[768,256]{1,0:T(8,128)(2,1)} %bitcast.4, bf16[9,256,256]{2,1,0:T(8,128)(2,1)} %wgt_in.1), custom_call_target="tpu_custom_call" | custom-call | flops 22000001024 | bytes 8000000 | tf_op jit(solution)/shard_map/deform_backward/pallas_call | solution.py:414
  53.9 1.8 %hand_out.1 = (bf16[24,32,256]{2,1,0:T(8,128)(2,1)}, f32[32,72]{1,0:T(8,128)}) custom-call(bf16[24,32,256]{2,1,0:T(8,128)(2,1)} %get-tuple-element.4.gx_in, f32[32,72]{1,0:T(8,128)} %get-tuple-element.5.gw_in), custom_call_target="tpu_custom_call" | custom-call | tf_op jit(solution)/shard_map/hand_out/pallas_call | solution.py:473

commit v5 on v4

--- a/solution.py
+++ b/solution.py
@@ -232,21 +232,22 @@
             fth[s, :, 2 * WC * q : 2 * WC * q + 2 * WC] = turned(rows[2 * q : 2 * q + 2])
         fth[s, :, len(rows) * WC :] = edges
 
-    def sibling_copy(k):
-        return remote(gbuf.at[k, 1 - core], rbuf.at[k], s1_send.at[k], s1_recv.at[k], (sibling, me_c))
-
-    def col_copy(k, d):
+    def sibling_copy(t):
+        return remote(gbuf.at[t, 1 - core], rbuf.at[t], s1_send.at[t], s1_recv.at[t], (sibling, me_c))
+
+    def col_copy(t, d):
         to = mod(me_c + d, NCOL)
-        return remote(sbuf.at[k, to], cbuf.at[k, d - 1], s2_send.at[k, d - 1], s2_recv.at[k, d - 1], (me_r, to))
-
-    def pass_on(k):
-        sibling_copy(k).wait_recv()
-        both = gbuf[k, core] + rbuf[k]
-        rbuf[k] = both
-        sbuf[k] = both.astype(BF16)
+        return remote(sbuf.at[t, to], cbuf.at[t, d - 1], s2_send.at[t, d - 1], s2_recv.at[t, d - 1], (me_r, to))
+
+    def pass_on(t):
+        sibling_copy(t).wait_recv()
+        for j in range(3):
+            both = gbuf[t, core, j] + rbuf[t, j]
+            rbuf[t, j] = both
+            sbuf[t, :, j] = both.astype(BF16)
 
         def send(d, carry):
-            col_copy(k, d).start()
+            col_copy(t, d).start()
             return carry
 
         lax.fori_loop(1, NCOL, send, 0)
@@ -283,26 +284,23 @@
                 total = total + dot(fth[s, :, 256 * q : 256 * q + 256], rhs)
             col[k, :, 256 * s : 256 * s + 256] = total.astype(BF16)
 
-    def kernel_grad(k):
-        cut = dot(gt[...], col[k], NT).reshape(NCOL, 2, HALF, CH)
-        gbuf[k, 0] = cut[:, 0]
-        gbuf[k, 1] = cut[:, 1]
+    def kernel_grad(t, j):
+        cut = dot(gt[...], col[3 * t + j], NT).reshape(NCOL, 2, HALF, CH)
+        gbuf[t, 0, j] = cut[:, 0]
+        gbuf[t, 1, j] = cut[:, 1]
 
     def three_taps(t, carry):
-        a, b, c = 3 * t, 3 * t + 1, 3 * t + 2
-        columns(a)
-        columns(b)
-        kernel_grad(a)
-        columns(c)
-        kernel_grad(b)
-        kernel_grad(c)
-        for k in (a, b, c):
-            sibling_copy(k).start()
+        columns(3 * t)
+        columns(3 * t + 1)
+        kernel_grad(t, 0)
+        columns(3 * t + 2)
+        kernel_grad(t, 1)
+        kernel_grad(t, 2)
+        sibling_copy(t).start()
 
         @pl.when(t > 0)
         def _():
-            for k in (a, b, c):
-                pass_on(k - 3)
+            pass_on(t - 1)
 
         return carry
 
@@ -313,20 +311,19 @@
 
         @pl.when(s == 0)
         def _():
-            for k in range(6, 9):
-                pass_on(k)
+            pass_on(2)
 
         return carry
 
     lax.fori_loop(0, 3, scatter_own, 0)
     fold_rows()
 
-    def gather_cols(k, carry):
-        total = rbuf[k, me_c]
+    def gather_cols(t, carry):
+        total = rbuf[t, :, me_c]
         for d in range(1, NCOL):
-            col_copy(k, d).wait_recv()
-            total = total + cbuf[k, d - 1].astype(F32)
-        own[k] = total
+            col_copy(t, d).wait_recv()
+            total = total + cbuf[t, d - 1].astype(F32)
+        own[t] = total
         return carry
 
     def row_copy(d):
@@ -348,11 +345,11 @@
         lax.fori_loop(first, last, send_row, 0)
 
     early = EARLY * CH // BLOCK
-    lax.fori_loop(0, EARLY, gather_cols, 0)
-    flat = [own[k] for k in range(EARLY)] + [jnp.zeros((HALF, 128), F32)]
+    lax.fori_loop(0, EARLY // 3, gather_cols, 0)
+    flat = [own[k // 3, k % 3] for k in range(EARLY)] + [jnp.zeros((HALF, 128), F32)]
     send_blocks(0, early, jnp.concatenate(flat, axis=1), 0)
-    lax.fori_loop(EARLY, TAPS, gather_cols, 0)
-    flat = [own[k] for k in range(EARLY - 1, TAPS)] + [jnp.zeros((HALF, 128), F32)]
+    gather_cols(2, 0)
+    flat = [own[k // 3, k % 3] for k in range(EARLY - 1, TAPS)] + [jnp.zeros((HALF, 128), F32)]
     send_blocks(early, NROW, jnp.concatenate(flat, axis=1), (EARLY - 1) * CH)
 
     g_copies[2].wait_recv()
@@ -371,8 +368,19 @@
 
     lax.fori_loop(0, TR, finish, 0)
 
+    for copy in f_copies + g_copies:
+        copy.wait_send()
+
+    def drain(t, carry):
+        sibling_copy(t).wait_send()
+        for d in range(1, NCOL):
+            col_copy(t, d).wait_send()
+        return carry
+
+    lax.fori_loop(0, 3, drain, 0)
+
     def gather_rows(d, carry):
-        row_copy(d).wait_recv()
+        row_copy(d).wait()
         same, other = carry
         piece = dbuf[d - 1].astype(F32)
         odd = lax.rem(d, 2) == 1
@@ -384,23 +392,6 @@
     scale = 1.0 / math.sqrt(float(NROW * TR * NCOL * TC))
     gw[0:HALF] = jnp.where(core == 0, same, other)[:, :BLOCK] * scale
     gw[HALF : 2 * HALF] = jnp.where(core == 0, other, same)[:, :BLOCK] * scale
-
-    for copy in f_copies + g_copies:
-        copy.wait_send()
-
-    def drain(k, carry):
-        sibling_copy(k).wait_send()
-        for d in range(1, NCOL):
-            col_copy(k, d).wait_send()
-        return carry
-
-    lax.fori_loop(0, TAPS, drain, 0)
-
-    def drain_row(d, carry):
-        row_copy(d).wait_send()
-        return carry
-
-    lax.fori_loop(1, NROW, drain_row, 0)
 
 
 def hand_out(gx_in, gw_in, gx, gw):
@@ -447,15 +438,15 @@
             pltpu.VMEM((2, 32, CH), F32),
             pltpu.VMEM((2, TR * 16 + 32, CH), BF16),
             pltpu.VMEM((2, TR * 16 + 32, CH), BF16),
-            pltpu.VMEM((TAPS, 2, NCOL, HALF, CH), F32),
-            pltpu.VMEM((TAPS, NCOL, HALF, CH), F32),
-            pltpu.VMEM((TAPS, HALF, CH), F32),
-            pltpu.VMEM((TAPS, NCOL, HALF, CH), BF16),
-            pltpu.VMEM((TAPS, NCOL - 1, HALF, CH), BF16),
+            pltpu.VMEM((3, 2, 3, NCOL, HALF, CH), F32),
+            pltpu.VMEM((3, 3, NCOL, HALF, CH), F32),
+            pltpu.VMEM((3, 3, HALF, CH), F32),
+            pltpu.VMEM((3, NCOL, 3, HALF, CH), BF16),
+            pltpu.VMEM((3, NCOL - 1, 3, HALF, CH), BF16),
             pltpu.VMEM((NROW, HALF, 128), BF16),
             pltpu.VMEM((NROW - 1, HALF, 128), BF16),
             dma((12,)), dma((12,)), dma((4,)), dma((4,)),
-            dma((TAPS,)), dma((TAPS,)), dma((TAPS, NCOL - 1)), dma((TAPS, NCOL - 1)),
+            dma((3,)), dma((3,)), dma((3, NCOL - 1)), dma((3, NCOL - 1)),
             dma((NROW - 1,)), dma((NROW - 1,)),
         ],
         compiler_params=pltpu.CompilerParams(

time: 56.2 us -> 54.6 us (0.972)
  Pallas kernels: 55.1 us -> 53.8 us
    pallas_call x1, Pallas kernels: 53.3 us -> 52.1 us  [body(): pl.pallas_call(kernel, name='deform_backward', out_shape=(jax.ShapeDtypeS...]
where the time goes in v5:
time: 54.6 us; the launch traced here: 54.5 us
  Pallas kernels  53.8 us (99%)
  between operations  0.64 us (1%)
    pallas_call x1, Pallas kernels, body(): pl.pallas_call(kernel, name='deform_backward', out_shape=(jax.ShapeDtypeS...  52.1 us
    pallas_call x1, Pallas kernels, body(): pl.pallas_call(hand_out, name='hand_out', out_shape=tuple((jax.ShapeDtype...  1.77 us

profile of v5, /device:TPU:1, one launch (start us, length us, event | category | flops | bytes accessed | tf_op | source)
XLA Modules:
  0.0 54.5 jit_solution(13541077335172244343)
XLA Ops:
  0.6 52.1 %deform_backward.1 = (bf16[24,32,256]{2,1,0:T(8,128)(2,1)}, f32[32,72]{1,0:T(8,128)}) custom-call(s32[2,216,32]{2,1,0:T(8,128)} %bitcast.5, f32[2,216,32]{2,1,0:T(8,128)} %bitcast.6, f32[1,216,32]{2,1,0:T(8,128)} %bitcast.7, bf16[24,32,256]{2,1,0:T(8,128)(2,1)} %feat.1, bf16[768,256]{1,0:T(8,128)(2,1)} %bitcast.4, bf16[9,256,256]{2,1,0:T(8,128)(2,1)} %wgt_in.1), custom_call_target="tpu_custom_call" | custom-call | flops 22000001024 | bytes 8000000 | tf_op jit(solution)/shard_map/deform_backward/pallas_call | solution.py:405
  52.7 1.8 %hand_out.1 = (bf16[24,32,256]{2,1,0:T(8,128)(2,1)}, f32[32,72]{1,0:T(8,128)}) custom-call(bf16[24,32,256]{2,1,0:T(8,128)(2,1)} %get-tuple-element.4.gx_in, f32[32,72]{1,0:T(8,128)} %get-tuple-element.5.gw_in), custom_call_target="tpu_custom_call" | custom-call | tf_op jit(solution)/shard_map/hand_out/pallas_call | solution.py:464

commit v6 on v5

--- a/solution.py
+++ b/solution.py
@@ -64,22 +64,6 @@
             src_ref=src, dst_ref=dst, send_sem=send, recv_sem=recv, device_id=device, device_id_type=MESH
         )
 
-    barrier = pltpu.get_barrier_semaphore()
-
-    def greet_row(d, carry):
-        pl.semaphore_signal(barrier, inc=1, device_id=(mod(me_r + d, NROW), me_c), device_id_type=MESH)
-        return carry
-
-    def greet_col(d, carry):
-        pl.semaphore_signal(barrier, inc=1, device_id=(me_r, mod(me_c + d, NCOL)), device_id_type=MESH)
-        return carry
-
-    for d in (1, -1):
-        greet_row(d, 0)
-        greet_col(d, 0)
-    lax.fori_loop(2, NCOL - 1, greet_col, 0)
-    lax.fori_loop(2, NROW - 1, greet_row, 0)
-
     home = fwin.at[pl.ds(RIM, TR), pl.ds(16, TC)]
     loads = [
         pltpu.make_async_copy(src, dst, in_sem.at[n])
@@ -89,6 +73,22 @@
     ]
     for load in loads:
         load.start()
+
+    barrier = pltpu.get_barrier_semaphore()
+
+    def greet_row(d, carry):
+        pl.semaphore_signal(barrier, inc=1, device_id=(mod(me_r + d, NROW), me_c), device_id_type=MESH)
+        return carry
+
+    def greet_col(d, carry):
+        pl.semaphore_signal(barrier, inc=1, device_id=(me_r, mod(me_c + d, NCOL)), device_id_type=MESH)
+        return carry
+
+    for d in (1, -1):
+        greet_row(d, 0)
+        greet_col(d, 0)
+    lax.fori_loop(2, NCOL - 1, greet_col, 0)
+    lax.fori_loop(2, NROW - 1, greet_row, 0)
 
     f_copies = [
         remote(feat.at[:, pl.ds(16, 16)], fwin.at[pl.ds(RIM, TR), pl.ds(0, 16)], f_send.at[0], f_recv.at[0], (me_r, right)),
@@ -306,17 +306,35 @@
 
     lax.fori_loop(0, 3, three_taps, 0)
 
-    def scatter_own(s, carry):
-        acc[rim : rim + TR * WC] = acc[rim : rim + TR * WC] + scatter(None, s, OWN_ROWS)
-
-        @pl.when(s == 0)
+    def scatter_half(s, first, second):
+        total = None
+        for k in range(TAPS):
+            ks = 3 * k + s
+            c = jnp.concatenate([c_ref[ks, first : first + 16, :], c_ref[ks, second : second + 16, :]], axis=0)
+            cells = [(r_ref[ks, i : i + 1, :] * c).astype(BF16) for i in OWN_ROWS]
+            part = dot(jnp.concatenate(cells, axis=0), gcol[k, strip_of(s), :])
+            total = part if total is None else total + part
+        for n, i in enumerate(OWN_ROWS):
+            for at, source in ((first, 32 * n), (second, 32 * n + 16)):
+                cells = slice(WC * i + at, WC * i + at + 16)
+                acc[cells, :] = acc[cells, :] + total[source : source + 16]
+
+    def scatter_outer(s, carry):
+        scatter_half(s, 0, 48)
+
+        @pl.when(s == 1)
         def _():
             pass_on(2)
 
         return carry
 
-    lax.fori_loop(0, 3, scatter_own, 0)
+    def scatter_inner(s, carry):
+        scatter_half(s, 16, 32)
+        return carry
+
+    lax.fori_loop(0, 3, scatter_outer, 0)
     fold_rows()
+    lax.fori_loop(0, 3, scatter_inner, 0)
 
     def gather_cols(t, carry):
         total = rbuf[t, :, me_c]

time: 54.6 us -> 52.6 us (0.963)
  Pallas kernels: 53.8 us -> 51.9 us
    pallas_call x1, Pallas kernels: 52.1 us -> 50.1 us  [body(): pl.pallas_call(kernel, name='deform_backward', out_shape=(jax.ShapeDtypeS...]
where the time goes in v6:
time: 52.6 us; the launch traced here: 52.5 us
  Pallas kernels  51.9 us (99%)
  between operations  0.64 us (1%)
    pallas_call x1, Pallas kernels, body(): pl.pallas_call(kernel, name='deform_backward', out_shape=(jax.ShapeDtypeS...  50.1 us
    pallas_call x1, Pallas kernels, body(): pl.pallas_call(hand_out, name='hand_out', out_shape=tuple((jax.ShapeDtype...  1.77 us

profile of v6, /device:TPU:1, one launch (start us, length us, event | category | flops | bytes accessed | tf_op | source)
XLA Modules:
  0.0 52.5 jit_solution(14756113385091094442)
XLA Ops:
  0.6 50.1 %deform_backward.1 = (bf16[24,32,256]{2,1,0:T(8,128)(2,1)}, f32[32,72]{1,0:T(8,128)}) custom-call(s32[2,216,32]{2,1,0:T(8,128)} %bitcast.5, f32[2,216,32]{2,1,0:T(8,128)} %bitcast.6, f32[1,216,32]{2,1,0:T(8,128)} %bitcast.7, bf16[24,32,256]{2,1,0:T(8,128)(2,1)} %feat.1, bf16[768,256]{1,0:T(8,128)(2,1)} %bitcast.4, bf16[9,256,256]{2,1,0:T(8,128)(2,1)} %wgt_in.1), custom_call_target="tpu_custom_call" | custom-call | flops 22000001024 | bytes 8000000 | tf_op jit(solution)/shard_map/deform_backward/pallas_call | solution.py:423
  50.7 1.8 %hand_out.1 = (bf16[24,32,256]{2,1,0:T(8,128)(2,1)}, f32[32,72]{1,0:T(8,128)}) custom-call(bf16[24,32,256]{2,1,0:T(8,128)(2,1)} %get-tuple-element.4.gx_in, f32[32,72]{1,0:T(8,128)} %get-tuple-element.5.gw_in), custom_call_target="tpu_custom_call" | custom-call | tf_op jit(solution)/shard_map/hand_out/pallas_call | solution.py:482

commit v7 on v6

--- a/solution.py
+++ b/solution.py
@@ -198,8 +198,6 @@
         copy.wait_recv()
     for copy in f_copies[6:]:
         copy.start()
-    g_copies[0].start()
-    g_copies[1].start()
 
     def turned(rows):
         pair = jnp.concatenate([fwin[rows[0]], fwin[rows[1]]], axis=0)
@@ -221,6 +219,8 @@
 
     for copy in f_copies[4:]:
         copy.wait_recv()
+    g_copies[0].start()
+    g_copies[1].start()
     at = iota((128, 192), 0)
     side, i = lax.div(at, 64), lax.rem(at, 64)
     slot = jnp.where(i < RIM, 64 + 7 + i, jnp.where(i < RIM + TR, i - RIM, 128 + i - RIM - TR)) + 32 * side

time: 52.6 us -> 59.1 us (1.12)
  Pallas kernels: 51.9 us -> 58.4 us
    pallas_call x1, Pallas kernels: 50.1 us -> 56.6 us  [body(): pl.pallas_call(kernel, name='deform_backward', out_shape=(jax.ShapeDtypeS...]
where the time goes in v7:
time: 59.1 us; the launch traced here: 59 us
  Pallas kernels  58.4 us (99%)
  between operations  0.64 us (1%)
    pallas_call x1, Pallas kernels, body(): pl.pallas_call(kernel, name='deform_backward', out_shape=(jax.ShapeDtypeS...  56.6 us
    pallas_call x1, Pallas kernels, body(): pl.pallas_call(hand_out, name='hand_out', out_shape=tuple((jax.ShapeDtype...  1.77 us

profile of v7, /device:TPU:1, one launch (start us, length us, event | category | flops | bytes accessed | tf_op | source)
XLA Modules:
  0.0 59.0 jit_solution(426716834862294268)
XLA Ops:
  0.6 56.6 %deform_backward.1 = (bf16[24,32,256]{2,1,0:T(8,128)(2,1)}, f32[32,72]{1,0:T(8,128)}) custom-call(s32[2,216,32]{2,1,0:T(8,128)} %bitcast.5, f32[2,216,32]{2,1,0:T(8,128)} %bitcast.6, f32[1,216,32]{2,1,0:T(8,128)} %bitcast.7, bf16[24,32,256]{2,1,0:T(8,128)(2,1)} %feat.1, bf16[768,256]{1,0:T(8,128)(2,1)} %bitcast.4, bf16[9,256,256]{2,1,0:T(8,128)(2,1)} %wgt_in.1), custom_call_target="tpu_custom_call" | custom-call | flops 22000001024 | bytes 8000000 | tf_op jit(solution)/shard_map/deform_backward/pallas_call | solution.py:423
  57.3 1.8 %hand_out.1 = (bf16[24,32,256]{2,1,0:T(8,128)(2,1)}, f32[32,72]{1,0:T(8,128)}) custom-call(bf16[24,32,256]{2,1,0:T(8,128)(2,1)} %get-tuple-element.4.gx_in, f32[32,72]{1,0:T(8,128)} %get-tuple-element.5.gw_in), custom_call_target="tpu_custom_call" | custom-call | tf_op jit(solution)/shard_map/hand_out/pallas_call | solution.py:482
